TPU v7x, 32 devices: a whole 2x2x4 slice. The times are simulated.
32 devices in a mesh: groups: 2 (over y), row: 8 (over z, x), col: 2 (over core).
Axes of the slice: x: 2, y: 2, z: 4, core: 2. Of those that a mesh axis runs over, the one named last changes fastest.
Arguments:
- wavenumber: float32 [2], P('groups'), parts along dimension 0, may hold values from 30 to 90
- tgt_geom: float32 [6, 4096], P(None, ('groups', 'row')), parts along dimension 1, may hold values from -2 to 8, as said below
- src_geom: float32 [4, 512], P(None, ('groups', 'row', 'col')), parts along dimension 1, may hold values from -2 to 8, as said below
- excite: bfloat16 [128, 512], P(None, ('groups', 'row', 'col')), parts along dimension 1, may hold values from -6 to 6
- tgt_nodes: float32 [3, 6144], P(None, ('groups', 'row')), parts along dimension 1, may hold values from -2 to 8, as said below
- src_nodes: float32 [3, 3072], P(None, ('groups', 'row')), parts along dimension 1, may hold values from -2 to 8, as said below
- tgt_weights: bfloat16 [2, 192, 4096], P(None, None, ('groups', 'row')), parts along dimension 2, may hold values from -0.109375 to 0.109375
- src_weights: bfloat16 [2, 192, 512], P(None, None, ('groups', 'row', 'col')), parts along dimension 2, may hold values from -1 to 1
- near_order: int32 [32, 9], P(('groups', 'row')), parts along dimension 0, may hold values from 0 to 3
Outputs:
- responses: float32 [4096, 128], P(('groups', 'row', 'col')), parts along dimension 0
There are 2 independent parts, one for each index of `groups`. A program takes and returns all parts, laid end to end along the dimension named above; each array names one. Nothing has to cross between parts.
Inputs may be any that keep to these rules, and one draw needn't show every extreme that they name: `tgt_geom`: rows 0 to 2 are points, rows 3 to 5 unit normals. `src_geom`: rows 0 to 2 are points, row 3 positive areas. `tgt_nodes`: Points. `src_nodes`: Points. `near_order`: 0 marks a pair that is not near.
All inputs are finite; a program needn't handle non-finite values.
Results may differ from a plain program's by a relative error of at most 0.0011.
Values may be sent and summed in bfloat16 or wider, within the bound.
No kernel may reach another device: no remote copies, remote signals or barrier semaphores. Data moves between devices by JAX's collectives and lax.ppermute only.
A program may use at most 64 MiB of HBM per device.

v0:
```python
import functools
import math

import jax
import jax.numpy as jnp
from jax import lax
from jax.experimental import pallas as pl
from jax.experimental.pallas import tpu as pltpu
from jax.sharding import PartitionSpec as P

QSTEP = 64
QN = 192
LANES = 128
PARTS = 3
SOFT = 0.05
INV_FOUR_PI = 1.0 / (4.0 * math.pi)
INV_TURN = 1.0 / (2.0 * math.pi)
TURN_HIGH = 6.28125
TURN_LOW = 2.0 * math.pi - TURN_HIGH
SIN_HALF = (3.14159264, -5.16771009, 2.55007766, -0.59829216, 0.07765941)
COS_HALF = (1.0, -4.93480214, 4.05870916, -1.33521206, 0.23493756, -0.02439672)
COS_FULL = (
    0.99999999, -19.73920453, 64.93911898, -85.45016555, 60.16783171, -25.96831321, 6.52961029
)
BF16 = jnp.bfloat16
F32 = jnp.float32
NN = (((1,), (0,)), ((), ()))
NT = (((1,), (1,)), ((), ()))
EXC_AT = 2 * QN
NODE_WIDTH = LANES
SMALL = pltpu.CompilerParams(vmem_limit_bytes=24 * 2**20)


def dot(left, right, dims=NN):
    return lax.dot_general(left, right, dims, preferred_element_type=F32)


def polynomial(z, coefficients):
    total = coefficients[-1]
    for c in coefficients[-2::-1]:
        total = total * z + c
    return total


def sincos_turns(f):
    z = f * f
    s = f * polynomial(z, SIN_HALF)
    c = polynomial(z, COS_HALF)
    twice = s + s
    return twice * c, 1.0 - twice * s


def three_parts(x):
    first = x.astype(BF16)
    rest = x - first.astype(F32)
    second = rest.astype(BF16)
    third = (rest - second.astype(F32)).astype(BF16)
    return first, second, third


def two_parts(x):
    first = x.astype(BF16)
    return first, (x - first.astype(F32)).astype(BF16)


def exchange_steps(count):
    bits = [1 << b for b in range(count.bit_length() - 2, 0, -1)]
    swapped = bits[:-2] + bits[-2:][::-1] if len(bits) >= 2 else bits
    return [b | 1 for b in bits], [b | 1 for b in swapped]


def relative_places(steps):
    places = [0]
    for step in steps:
        places = places + [p ^ step for p in places]
    return places


def iota(shape, axis):
    return lax.broadcasted_iota(jnp.int32, shape, axis)


def geom_lane(cpd):
    return 3 * PARTS * (QN // cpd)


def place_matrices(cpd):
    groups = QN // cpd
    shape = (LANES, 2 * 16)
    begin, row = iota(shape, 0), iota(shape, 1)
    node = jnp.logical_and(begin >= row * groups, begin < (row + 1) * groups)
    node = jnp.logical_and(node, row < 3 * PARTS)
    source = jnp.logical_and(begin - geom_lane(cpd) == row - 16, row >= 16)
    row_of = jnp.where(jnp.logical_or(node, source), 1.0, 0.0).astype(BF16)
    shape = (LANES, QN)
    lane, group = iota(shape, 0), lax.div(iota(shape, 1), cpd)
    wanted = jnp.where(lane < geom_lane(cpd), lax.rem(lane, groups), 0)
    kept = jnp.where(group == wanted, 1.0, 0.0)
    shape = (cpd, QN)
    column_of = jnp.where(lax.rem(iota(shape, 1), cpd) == iota(shape, 0), 1.0, 0.0).astype(BF16)
    return row_of, kept, column_of


def pack_kernel(
    units, order_hbm, geom_hbm, excite_hbm, nodes_hbm, weights_hbm, tnodes_hbm, tweights_hbm,
    out_ref, target_ref, tests_ref, found_ref,
    order_ref, geom_ref, excite_ref, nodes_ref, weights_ref, tnodes_ref, arrived,
):
    col = lax.axis_index("col")
    rows = tests_ref.shape[2]
    at = pl.ds(pl.multiple_of(col * rows, LANES), rows)
    moves = [
        (weights_hbm, weights_ref),
        (nodes_hbm, nodes_ref),
        (geom_hbm, geom_ref),
        (excite_hbm, excite_ref),
        (tnodes_hbm, tnodes_ref),
        (order_hbm, order_ref),
        (tweights_hbm.at[:, :, at], tests_ref),
    ]
    copies = [pltpu.make_async_copy(*move, arrived.at[i]) for i, move in enumerate(moves)]
    for copy in copies:
        copy.start()
    cpd, exc = excite_ref.shape
    row_of, kept, column_of = place_matrices(cpd)
    for copy in copies[:-1]:
        copy.wait()
    main = LANES
    rest = QN - main
    re, im = weights_ref[0], weights_ref[1]
    out_ref[:, 0:main] = re[:, :main]
    out_ref[:, main : 2 * main] = im[:, :main]
    out_ref[:, 2 * main : 2 * main + 2 * rest] = jnp.concatenate([re[:, main:], im[:, main:]], 1)
    out_ref[:, EXC_AT : EXC_AT + exc] = excite_ref[...]
    nodes = [p.astype(F32) for p in three_parts(nodes_ref[...])]
    geom = jnp.concatenate([p.astype(F32) for p in three_parts(geom_ref[...])], 0)
    values = jnp.concatenate(
        nodes
        + [
            jnp.zeros((16 - 3 * PARTS, QN), F32),
            jnp.concatenate([geom, jnp.zeros((geom.shape[0], QN - cpd), F32)], 1),
            jnp.zeros((16 - geom.shape[0], QN), F32),
        ],
        0,
    ).astype(BF16)
    spread = (dot(row_of, values) * kept).astype(BF16)
    out_ref[:, EXC_AT + exc :] = dot(column_of, spread, NT).astype(BF16)
    nodes = tnodes_ref[:, :QN]
    for b in range(1, tnodes_ref.shape[1] // QN):
        nodes = jnp.where(col == b, tnodes_ref[:, b * QN : (b + 1) * QN], nodes)
    end = nodes[:, LANES:]
    start = nodes[:, :QSTEP]
    target_ref[0, 0:3] = nodes[:, :LANES]
    target_ref[1, 0:3] = jnp.concatenate([end, end], 1)
    target_ref[2, 0:3] = jnp.concatenate([start, start], 1)
    for slot, order in enumerate(slot_orders(order_ref, units)):
        found_ref[slot] = order
    copies[-1].wait()


def store_tests(tests_ref, ut_ref):
    re, im = tests_ref[0], tests_ref[1]
    main = LANES
    ut_ref[0:main, :] = jnp.concatenate([re[:main], im[:main]], 1)
    ut_ref[main : 2 * main, :] = jnp.concatenate([-im[:main], re[:main]], 1)
    ut_ref[2 * main : 2 * main + QSTEP, :] = jnp.concatenate([re[main:], im[main:]], 1)
    ut_ref[2 * main + QSTEP :, :] = jnp.concatenate([-im[main:], re[main:]], 1)


def node_columns(data_ref, exc):
    block = data_ref[:, EXC_AT + exc :].astype(F32)
    step = geom_lane(16) // PARTS
    return (block[:, :step] + block[:, step : 2 * step]) + block[:, 2 * step : 3 * step]


def two_part_dot(high, low, right):
    count = high.shape[0]
    both = dot(jnp.concatenate([high, low], 0), right)
    return both[:count] + both[count:]


def near_slot(order, columns, slot, target_ref, ut_ref, turns, out_ref):
    lane = lax.broadcasted_iota(jnp.int32, (1, LANES), 1)
    quarter = jnp.where(lane < QSTEP, 0.0, 0.25)
    main = LANES

    def located(count):
        return [
            jnp.concatenate(
                [
                    jnp.broadcast_to(columns[16 * slot : 16 * slot + 16, lane : lane + 1], (16, LANES))
                    for lane in range(axis * (QN // 16), axis * (QN // 16) + count // 16)
                ],
                0,
            )
            for axis in range(3)
        ]

    def distance2(source, tile):
        total = SOFT * SOFT
        for axis in range(3):
            d = source[axis] - target_ref[tile, axis : axis + 1, :]
            total = total + d * d
        return total

    def both(source):
        d2 = distance2(source, 0)
        inv = lax.rsqrt(d2)
        t = (d2 * inv) * turns
        sin, cos = sincos_turns(t - jnp.round(t))
        return two_parts(inv * cos), two_parts(inv * sin)

    def split_lanes(source, tile):
        d2 = distance2(source, tile)
        inv = lax.rsqrt(d2)
        t = (d2 * inv) * turns
        f = (t - jnp.round(t - quarter)) - quarter
        return two_parts(inv * polynomial(f * f, COS_FULL))

    def put(at, value):
        high, low = two_parts(value)
        count = value.shape[0]
        out_ref[at : at + count, :LANES] = high
        out_ref[at : at + count, LANES:] = low

    def clear(begin, end):
        out_ref[begin:end, :] = jnp.zeros((end - begin, 2 * LANES), BF16)

    @pl.when(order == 3)
    def _():
        source = located(QN)
        (re_high, re_low), (im_high, im_low) = both(source)
        rest_high, rest_low = split_lanes(source, 1)
        high = jnp.concatenate([re_high, im_high, rest_high], 1)
        low = jnp.concatenate([re_low, im_low, rest_low], 1)
        v = two_part_dot(high, low, ut_ref[...])
        put(0, v[:main, :LANES])
        put(main, v[:main, LANES:])
        put(2 * main, v[main:, :LANES])
        put(2 * main + QSTEP, v[main:, LANES:])

    @pl.when(order == 2)
    def _():
        (re_high, re_low), (im_high, im_low) = both(located(main))
        high = jnp.concatenate([re_high, im_high], 1)
        low = jnp.concatenate([re_low, im_low], 1)
        v = two_part_dot(high, low, ut_ref[: 2 * main])
        put(0, v[:, :LANES])
        put(main, v[:, LANES:])
        clear(2 * main, 3 * main)

    @pl.when(order == 1)
    def _():
        high, low = split_lanes(located(QSTEP), 2)
        weights = jnp.concatenate([ut_ref[0:QSTEP], ut_ref[main : main + QSTEP]], 0)
        v = two_part_dot(high, low, weights)
        put(0, v[:, :LANES])
        clear(QSTEP, main)
        put(main, v[:, LANES:])
        clear(main + QSTEP, 3 * main)

    @pl.when(order == 0)
    def _():
        clear(0, 3 * main)


def slot_orders(order_ref, units):
    row, col = lax.axis_index("row"), lax.axis_index("col")
    nrow = lax.axis_size("row")
    band = order_ref.shape[1]
    reach = (band - 1) // 2
    if units is None:
        offsets = [jnp.where(jnp.logical_and(row + o >= reach, row + o - reach < nrow), o, -1) for o in range(band)]
    else:
        place, parity = row * lax.axis_size("col") + col, 0
        for _ in range((nrow * lax.axis_size("col")).bit_length() - 1):
            parity = parity + lax.rem(place, 2)
            place = lax.div(place, 2)
        parity = lax.rem(parity, 2)
        offsets = [
            (row ^ (a if a == b else jnp.where(parity == 0, a, b))) - row + reach for a, b in zip(*units)
        ]
    return [
        jnp.where(
            jnp.logical_and(o >= 0, o < band), order_ref[col, jnp.clip(o, 0, band - 1)], 0
        )
        for o in offsets
    ]


def far_kernel_values(wave, source, tgeom):
    dx = tgeom[0:1] - source[0]
    dy = tgeom[1:2] - source[1]
    dz = tgeom[2:3] - source[2]
    d2 = dx * dx + dy * dy + dz * dz + SOFT * SOFT
    inv = lax.rsqrt(d2)
    radius = d2 * inv
    cosine = (tgeom[3:4] * dx + tgeom[4:5] * dy + tgeom[5:6] * dz) * inv
    scale = source[3] * (INV_FOUR_PI * inv)
    phase = wave * radius
    t = phase * INV_TURN
    n = jnp.round(t)
    sin, cos = sincos_turns(((phase - n * TURN_HIGH) - n * TURN_LOW) * INV_TURN)
    green_re = scale * cos
    green_im = scale * sin
    factor_re = 1.0 - cosine
    factor_im = cosine * (inv * (-1.0 / wave))
    kern_re = (green_re * factor_re - green_im * factor_im).astype(BF16)
    kern_im = (green_re * factor_im + green_im * factor_re).astype(BF16)
    return kern_re, kern_im


def far_rows(data, exc, wave, tgeom):
    shape = (LANES, 4 * LANES)
    at, wanted = iota(shape, 0) - geom_lane(16), lax.div(iota(shape, 1), LANES)
    pick = jnp.logical_and(
        jnp.logical_and(at >= 0, at < 4 * PARTS), lax.rem(at + 4 * LANES, 4) == wanted
    )
    geom = data[:, EXC_AT + exc :]
    spread = dot(geom, jnp.where(pick, 1.0, 0.0).astype(BF16))
    return far_kernel_values(wave, [spread[:, i * LANES : (i + 1) * LANES] for i in range(4)], tgeom)


def own_targets(tgeom_ref, rows):
    at = pl.multiple_of(lax.axis_index("col") * rows, LANES)
    return tgeom_ref[:, pl.ds(at, rows)]


def near_kernel(
    exc, first, wave_ref, found_ref, data_ref, own_ref, target_ref, ut_ref, tgeom_ref,
    v_ref, kern_re_ref, kern_im_ref, *copy_ref,
):
    if copy_ref:
        copy_ref[0][...] = own_ref[...]
    wave = wave_ref[0]
    tgeom = own_targets(tgeom_ref, kern_re_ref.shape[1])
    data = data_ref[...]
    if kern_re_ref.shape[0] > data.shape[0]:
        data = jnp.concatenate([own_ref[...], data], 0)
    kern_re_ref[...], kern_im_ref[...] = far_rows(data, exc, wave, tgeom)
    slots = v_ref.shape[0]
    skipped = data_ref.shape[0] // 16 - slots
    columns = node_columns(data_ref, exc)
    for slot in range(slots):
        near_slot(
            found_ref[first + slot], columns, skipped + slot, target_ref, ut_ref, wave * INV_TURN, v_ref.at[slot]
        )


def first_near_kernel(
    exc, first, wave_ref, found_ref, data_ref, own_ref, target_ref, tests_ref, tgeom_ref, *refs
):
    *refs, ut_ref = refs
    store_tests(tests_ref, ut_ref)
    near_kernel(exc, first, wave_ref, found_ref, data_ref, own_ref, target_ref, ut_ref, tgeom_ref, *refs)


def last_kernel(
    exc, partner, wave_ref, own_early, own_late, other_first, other_early, other_late, tgeom_ref,
    early_re_ref, early_im_ref, *refs
):
    own = jnp.concatenate([own_early[...], own_late[...]], 0)
    other = jnp.concatenate([other_first[...], other_early[...], other_late[...]], 0)
    out_ref, zre, zim = refs[-3:]
    *made, early_v, late_v, late_re, late_im = refs[:-3]
    v_refs = [*made[::3], early_v, late_v]
    kern_re_refs, kern_im_refs = [*made[1::3], late_re], [*made[2::3], late_im]
    rows = out_ref.shape[0]
    cpd = 16
    main = LANES
    slots = len(partner)
    sign = jnp.where(lax.broadcasted_iota(jnp.int32, (1, LANES), 1) < QSTEP, 1.0, -1.0).astype(BF16)

    def weight_rows(data):
        w = [data[:, i * main : (i + 1) * main] for i in range(3)]
        swapped = jnp.concatenate([w[2][:, QSTEP:], w[2][:, :QSTEP]], 1)
        return jnp.concatenate([w[0], -w[1], w[2] * sign], 1), jnp.concatenate([w[1], w[0], swapped], 1)

    own_re, own_im = weight_rows(own)
    other_re, other_im = weight_rows(other)
    slot = 0
    for v_ref in v_refs:
        for i in range(v_ref.shape[0]):
            here = slice(slot * cpd, (slot + 1) * cpd)
            there = slice(partner[slot] * cpd, (partner[slot] + 1) * cpd)
            left = jnp.concatenate([own_re[here], other_re[there], own_im[here], other_im[there]], 0)
            product = dot(left, v_ref[i])
            a = (product[:, :LANES] + product[:, LANES:]) * INV_FOUR_PI
            there = slice((slots + partner[slot]) * cpd, (slots + partner[slot] + 1) * cpd)
            zre[here] = a[0:cpd]
            zre[there] = a[cpd : 2 * cpd]
            zim[here] = a[2 * cpd : 3 * cpd]
            zim[there] = a[3 * cpd :]
            slot += 1

    late_kern = far_rows(other_late, exc, wave_ref[0], own_targets(tgeom_ref, rows))
    other_kern = [
        jnp.concatenate([early[...], x], 0)
        for x, early in zip(late_kern, (early_re_ref, early_im_ref))
    ]
    kern_re, kern_im = [
        jnp.concatenate([ref[...] for ref in refs] + [last], 0).astype(F32)
        for refs, last in zip((kern_re_refs, kern_im_refs), other_kern)
    ]
    excite = jnp.concatenate(
        [own[:, EXC_AT : EXC_AT + exc], other[:, EXC_AT : EXC_AT + exc]], 0
    ).T
    re = two_parts(kern_re + zre[...])
    im = two_parts(kern_im + zim[...])
    product = dot(excite, jnp.concatenate([*re, *im], 1))
    by_re = product[:, :rows] + product[:, rows : 2 * rows]
    by_im = product[:, 2 * rows : 3 * rows] + product[:, 3 * rows :]
    h = exc // 2
    result = jnp.concatenate([by_re[:h] - by_im[h:], by_re[h:] + by_im[:h]], 0)
    out_ref[...] = result.T


def in_vmem(x):
    return pltpu.with_memory_space_constraint(x, pltpu.VMEM)


def in_smem(x):
    return pltpu.with_memory_space_constraint(x, pltpu.SMEM)


def in_hbm(x):
    return pltpu.with_memory_space_constraint(x, pltpu.HBM)


SMEM_SPEC = pl.BlockSpec(memory_space=pltpu.SMEM)
VMEM_SPEC = pl.BlockSpec(memory_space=pltpu.VMEM)


def packed(units, slots, src_geom, excite, src_nodes, src_weights, tgt_nodes, tgt_weights, near_order):
    excite = excite.T
    src_weights = src_weights.transpose(0, 2, 1)
    cpd, exc = excite.shape
    rows_here = tgt_weights.shape[2] // lax.axis_size("col")
    inputs = (near_order, src_geom, excite, src_nodes, src_weights, tgt_nodes)
    return pl.pallas_call(
        functools.partial(pack_kernel, units),
        out_shape=[
            pltpu.VMEM((cpd, EXC_AT + exc + NODE_WIDTH), BF16),
            pltpu.VMEM((3, 8, LANES), F32),
            pltpu.VMEM((2, QN, rows_here), BF16),
            pltpu.SMEM((slots,), jnp.int32),
        ],
        in_specs=[pl.BlockSpec(memory_space=pl.ANY)] * 7,
        out_specs=[VMEM_SPEC] * 3 + [SMEM_SPEC],
        scratch_shapes=[pltpu.SMEM(near_order.shape, jnp.int32)]
        + [pltpu.VMEM(x.shape, x.dtype) for x in inputs[1:]]
        + [pltpu.SemaphoreType.DMA((7,))],
        compiler_params=SMALL,
    )(*[in_hbm(x) for x in inputs], in_hbm(tgt_weights))


def near_blocks(exc, first, slots, wavenumber, found, fresh, own, target, ut, tgt_geom, hand_on, both=False):
    rows_here = tgt_geom.shape[1] // lax.axis_size("col")
    kern = pltpu.VMEM((fresh.shape[0] + both * own.shape[0], rows_here), BF16)
    cost = pl.CostEstimate(flops=1, bytes_accessed=1, transcendentals=0)
    outs = [pltpu.VMEM((slots, 2 * QN, 2 * LANES), BF16), kern, kern] + [pltpu.VMEM(own.shape, BF16)] * hand_on
    if first == 0:
        outs.append(pltpu.VMEM((2 * QN, 2 * LANES), BF16))
    return pl.pallas_call(
        functools.partial(near_kernel if first else first_near_kernel, exc, first),
        out_shape=outs,
        in_specs=[SMEM_SPEC] * 2 + [VMEM_SPEC] * 5,
        out_specs=[VMEM_SPEC] * len(outs),
        compiler_params=SMALL,
        cost_estimate=cost,
    )(wavenumber, in_smem(found), in_vmem(fresh), in_vmem(own), in_vmem(target), in_vmem(ut), in_vmem(tgt_geom))


def exchanged(
    wavenumber, tgt_geom, src_geom, excite, tgt_nodes, src_nodes, tgt_weights, src_weights, near_order
):
    cpd = src_geom.shape[1]
    exc = excite.shape[0]
    cores = lax.axis_size("col")
    count = cores * lax.axis_size("row")
    rows_here = tgt_geom.shape[1] // cores
    even, odd = exchange_steps(count)
    units = [[p >> 1 for p in relative_places(s)] for s in (even, odd)]
    own, target, ut, found = packed(
        units, len(units[0]), src_geom, excite, src_nodes, src_weights, tgt_nodes, tgt_weights, near_order
    )

    def moved(value, a, b):
        pairs = [(i, i ^ (b if bin(i).count("1") % 2 else a)) for i in range(count)]
        return lax.ppermute(value, ("row", "col"), pairs)

    fresh = own
    near = []
    done = 0
    steps = list(zip(even, odd))
    for step, (a, b) in enumerate(steps):
        arriving = moved(own, a, b)
        slots = fresh.shape[0] // cpd
        made = near_blocks(exc, done, slots, wavenumber, found, fresh, own, target, ut, tgt_geom, True)
        near.extend(made[:3])
        if not done:
            ut = made[4]
        if step == len(steps) - 2:
            other_first = moved(made[3], 1, 1)
        done += slots
        fresh = arriving
        if step < len(steps) - 1:
            own = jnp.concatenate([made[3], arriving], 0)
    half = own.shape[0] // 2
    other_early = moved(own[half:], 1, 1)
    quarter = half // cpd
    early = near_blocks(
        exc, done, quarter, wavenumber, found, other_early, other_first, target, ut, tgt_geom, False, True
    )
    fresh, early, made = lax.optimization_barrier((fresh, early, made))
    other_late = moved(fresh, 1, 1)
    late = near_blocks(
        exc, done + quarter, quarter, wavenumber, found, fresh, fresh, target, ut, tgt_geom, False
    )
    near.append(early[0])
    near.extend(late)
    partner = [units[1].index(u) for u in units[0]]
    return pl.pallas_call(
        functools.partial(last_kernel, exc, partner),
        out_shape=jax.ShapeDtypeStruct((rows_here, exc), F32),
        in_specs=[SMEM_SPEC] + [VMEM_SPEC] * (8 + len(near)),
        out_specs=VMEM_SPEC,
        scratch_shapes=[pltpu.VMEM((count * cpd, rows_here), F32)] * 2,
        compiler_params=SMALL,
    )(
        wavenumber,
        *[in_vmem(x) for x in (made[3], fresh, other_first, other_early, other_late, tgt_geom, *early[1:], *near)],
    )


def gathered(
    wavenumber, tgt_geom, src_geom, excite, tgt_nodes, src_nodes, tgt_weights, src_weights, near_order
):
    cpd = src_geom.shape[1]
    exc = excite.shape[0]
    half = exc // 2
    cores = lax.axis_size("col")
    nrow = lax.axis_size("row")
    row = lax.axis_index("row")
    rows_here = tgt_geom.shape[1] // cores
    band = near_order.shape[1]
    own, target, ut, found = packed(
        None, band, src_geom, excite, src_nodes, src_weights, tgt_nodes, tgt_weights, near_order
    )
    everything = lax.all_gather(own, ("row", "col"), axis=0, tiled=True)
    sources = lax.all_gather(src_geom, ("row", "col"), axis=1, tiled=True)
    blocks = [
        lax.dynamic_slice_in_dim(
            everything, jnp.clip(row + o - (band - 1) // 2, 0, nrow - 1) * cores * cpd, cores * cpd, 0
        )
        for o in range(band)
    ]
    fresh = jnp.concatenate([block[:cpd] for block in blocks], 0)
    near = near_blocks(exc, 0, band, wavenumber, found, fresh, own, target, ut, tgt_geom, False)[0]
    high = lax.Precision.HIGHEST
    total = jnp.zeros((rows_here, exc), F32)
    dims = (((0,), (0,)), ((), ()))
    m, r = LANES, QN - LANES
    for o, block in enumerate(blocks):
        w, x = block[:, :EXC_AT].astype(F32), block[:, EXC_AT : EXC_AT + exc].astype(F32)
        v = near[o, :, :LANES].astype(F32) + near[o, :, LANES:].astype(F32)
        w_re = jnp.concatenate([w[:, :m], w[:, 2 * m : 2 * m + r]], 1)
        w_im = jnp.concatenate([w[:, m : 2 * m], w[:, 2 * m + r :]], 1)
        v_re = jnp.concatenate([v[:m], v[2 * m : 2 * m + r]], 0)
        v_im = jnp.concatenate([v[m : 2 * m], v[2 * m + r :]], 0)
        a_re = jnp.dot(w_re, v_re, precision=high) - jnp.dot(w_im, v_im, precision=high)
        a_im = jnp.dot(w_re, v_im, precision=high) + jnp.dot(w_im, v_re, precision=high)
        re = lax.dot_general(a_re, x, dims, precision=high)
        im = lax.dot_general(a_im, x, dims, precision=high)
        total = total + INV_FOUR_PI * jnp.concatenate(
            [re[:, :half] - im[:, half:], re[:, half:] + im[:, :half]], 1
        )
    targets = lax.dynamic_slice_in_dim(tgt_geom, lax.axis_index("col") * rows_here, rows_here, 1)
    width = math.gcd(everything.shape[0], 512)

    def far(index, accum):
        places = lax.dynamic_slice_in_dim(sources, index * width, width, 1)
        x = lax.dynamic_slice_in_dim(everything, index * width, width, 0)[:, EXC_AT : EXC_AT + exc]
        kern_re, kern_im = far_kernel_values(
            wavenumber[0], [places[i][:, None] for i in range(4)], targets
        )
        re = lax.dot_general(kern_re.astype(BF16), x, dims, preferred_element_type=F32)
        im = lax.dot_general(kern_im.astype(BF16), x, dims, preferred_element_type=F32)
        return accum + jnp.concatenate([re[:, :half] - im[:, half:], re[:, half:] + im[:, :half]], 1)

    return lax.fori_loop(0, everything.shape[0] // width, far, total)


def on_device(*arguments):
    count = lax.axis_size("row") * lax.axis_size("col")
    short = lax.axis_size("col") == 2 and lax.axis_size("row") <= 16 and count & (count - 1) == 0
    return (exchanged if short and count >= 8 else gathered)(*arguments)


def solution(mesh):
    return jax.shard_map(
        on_device,
        mesh=mesh,
        in_specs=(
            P("groups"),
            P(None, ("groups", "row")),
            P(None, ("groups", "row", "col")),
            P(None, ("groups", "row", "col")),
            P(None, ("groups", "row")),
            P(None, ("groups", "row")),
            P(None, None, ("groups", "row")),
            P(None, None, ("groups", "row", "col")),
            P(("groups", "row"), None),
        ),
        out_specs=P(("groups", "row", "col"), None),
        check_vma=False,
    )
```

profile of v0, /device:TPU:0, one launch (start us, length us, event | category | flops | bytes accessed | tf_op | source)
XLA Modules:
  0.0 16.7 jit_solution(17848586332031000508)
XLA Ops:
  0.0 1.2 %shard_map.91 = (bf16[16,640]{1,0:T(8,128)(2,1)S(1)}, f32[3,8,128]{2,1,0:T(8,128)S(1)}, bf16[2,192,128]{2,1,0:T(8,128)(2,1)S(1)}, s32[8]{0:T(128)S(4)}) custom-call(s32[2,9]{1,0:T(2,128)} %order_hbm.1, f32[4,16]{1,0:T(4,128)} %geom_hbm.1, bf16[16,128]{1,0:T(8,128)(2,1)} %bitcast.3, f32[3,192]{1,0:T(4,128)} %nodes_hbm.1, bf16[2,16,192]{2,1,0:T(8,128)(2,1)} %bitcast.2, ...), custom_call_target="tpu_custom_call" | custom-call | tf_op jit(solution)/shard_map/pallas_call | solution.py:440
  1.2 0.0 copy-start
  1.2 3.5 %collective-permute-start = (bf16[16,640]{1,0:T(8,128)(2,1)S(1)}, bf16[16,640]{1,0:T(8,128)(2,1)S(1)}, u32[]{:S(2)}, u32[]{:S(2)}) collective-permute-start(bf16[16,640]{1,0:T(8,128)(2,1)S(1)} %get-tuple-element.34.data_ref.own_ref), channel_id=1, source_target_pairs={{0,9},{1,8},{2,11},{3,10},{4,13},{5,12},{6,15},{7,14},{8,1},{9,0},... | collective-permute-start | bytes 61448 | tf_op jit(solution)/shard_map/ppermute | solution.py:490
  5.4 0.0 copy-done
  5.4 0.4 %shard_map.92 = (bf16[1,384,256]{2,1,0:T(8,128)(2,1)S(1)}, bf16[16,128]{1,0:T(8,128)(2,1)S(1)}, bf16[16,128]{1,0:T(8,128)(2,1)S(1)}, bf16[16,640]{1,0:T(8,128)(2,1)S(1)}, bf16[384,256]{1,0:T(8,128)(2,1)S(1)}) custom-call(f32[1]{0:T(128)S(6)} %copy.12.wave_ref, s32[8]{0:T(128)S(4)} %get-tuple-element.33.found_ref, ...), custom_call_target="tpu_custom_call" | custom-call | flops 1 | bytes 1 | tf_op jit(solution)/shard_map/pallas_call | solution.py:464
  5.9 0.4 %collective-permute-done.data_ref = bf16[16,640]{1,0:T(8,128)(2,1)S(1)} collective-permute-done((bf16[16,640]{1,0:T(8,128)(2,1)S(1)}, bf16[16,640]{1,0:T(8,128)(2,1)S(1)}, u32[]{:S(2)}, u32[]{:S(2)}) %collective-permute-start) | collective-permute-done | bytes 20512 | tf_op jit(solution)/shard_map/ppermute | solution.py:490
  6.3 1.9 %collective-permute-start.1 = (bf16[32,640]{1,0:T(8,128)(2,1)S(1)}, bf16[32,640]{1,0:T(8,128)(2,1)S(1)}, u32[]{:S(2)}, u32[]{:S(2)}) collective-permute-start(bf16[32,640]{1,0:T(8,128)(2,1)S(1)} %constant_dynamic-update-slice_fusion.own_ref), channel_id=1, source_target_pairs={{0,5},{1,2},{2,1},{3,6},{4,7},{5,0},{6,3},{7,4},{8,11},{9,12},{10,... | collective-permute-start | bytes 122888 | tf_op jit(solution)/shard_map/ppermute | solution.py:490
  8.1 0.7 %shard_map.93 = (bf16[1,384,256]{2,1,0:T(8,128)(2,1)S(1)}, bf16[16,128]{1,0:T(8,128)(2,1)S(1)}, bf16[16,128]{1,0:T(8,128)(2,1)S(1)}, bf16[32,640]{1,0:T(8,128)(2,1)S(1)}) custom-call(f32[1]{0:T(128)S(6)} %copy.12.wave_ref, s32[8]{0:T(128)S(4)} %get-tuple-element.33.found_ref, bf16[16,640]{1,0:T(8,128)(2,1)S(1)} %collective-permute-done.data_ref, ...), custom_call_target="tpu_custom_call" | custom-call | flops 1 | bytes 1 | tf_op jit(solution)/shard_map/pallas_call | solution.py:464
  8.8 1.0 %collective-permute-done.1.data_ref = bf16[32,640]{1,0:T(8,128)(2,1)S(1)} collective-permute-done((bf16[32,640]{1,0:T(8,128)(2,1)S(1)}, bf16[32,640]{1,0:T(8,128)(2,1)S(1)}, u32[]{:S(2)}, u32[]{:S(2)}) %collective-permute-start.1) | collective-permute-done | bytes 40992 | tf_op jit(solution)/shard_map/ppermute | solution.py:490
  9.8 1.7 %collective-permute-start.2 = (bf16[64,640]{1,0:T(8,128)(2,1)S(1)}, bf16[64,640]{1,0:T(8,128)(2,1)S(1)}, u32[]{:S(2)}, u32[]{:S(2)}) collective-permute-start(bf16[64,640]{1,0:T(8,128)(2,1)S(1)} %constant_dynamic-update-slice_fusion.2.own_ref), channel_id=1, source_target_pairs={{0,3},{1,4},{2,7},{3,0},{4,1},{5,6},{6,5},{7,2},{8,13},{9,10},{10,... | collective-permute-start | bytes 245768 | tf_op jit(solution)/shard_map/ppermute | solution.py:490
  11.5 0.5 %collective-permute-start.4 = (bf16[32,640]{1,0:T(8,128)(2,1)S(1)}, bf16[32,640]{1,0:T(8,128)(2,1)S(1)}, u32[]{:S(2)}, u32[]{:S(2)}) collective-permute-start(bf16[32,640]{1,0:T(8,128)(2,1)S(1)} %get-tuple-element.39), channel_id=1, source_target_pairs={{0,1},{1,0},{2,3},{3,2},{4,5},{5,4},{6,7},{7,6},{8,9},{9,8},{10,11... | collective-permute-start | bytes 122888 | tf_op jit(solution)/shard_map/ppermute | solution.py:490
  12.0 0.0 collective-permute-start.3
  12.0 0.2 %shard_map.95 = (bf16[2,384,256]{2,1,0:T(8,128)(2,1)S(1)}, bf16[32,128]{1,0:T(8,128)(2,1)S(1)}, bf16[32,128]{1,0:T(8,128)(2,1)S(1)}, bf16[64,640]{1,0:T(8,128)(2,1)S(1)}) custom-call(f32[1]{0:T(128)S(6)} %copy.12.wave_ref, s32[8]{0:T(128)S(4)} %get-tuple-element.33.found_ref, bf16[32,640]{1,0:T(8,128)(2,1)S(1)} %collective-permute-done.1.data_ref, ...), custom_call_target="tpu_custom_call" | custom-call | flops 1 | bytes 1 | tf_op jit(solution)/shard_map/pallas_call | solution.py:464
  12.2 0.6 %collective-permute-done.4.own_ref.other_first = bf16[32,640]{1,0:T(8,128)(2,1)S(1)} collective-permute-done((bf16[32,640]{1,0:T(8,128)(2,1)S(1)}, bf16[32,640]{1,0:T(8,128)(2,1)S(1)}, u32[]{:S(2)}, u32[]{:S(2)}) %collective-permute-start.4) | collective-permute-done | bytes 40992 | tf_op jit(solution)/shard_map/ppermute | solution.py:490
  12.8 0.3 %collective-permute-done.3.data_ref.other_early = bf16[32,640]{1,0:T(8,128)(2,1)S(1)} collective-permute-done((bf16[32,640]{1,0:T(8,128)(2,1)S(1)}, bf16[32,640]{1,0:T(8,128)(2,1)S(1)}, u32[]{:S(2)}, u32[]{:S(2)}) %collective-permute-start.3) | collective-permute-done | bytes 40992 | tf_op jit(solution)/shard_map/ppermute | solution.py:490
  13.2 0.8 %shard_map.94 = (bf16[2,384,256]{2,1,0:T(8,128)(2,1)S(1)}, bf16[64,128]{1,0:T(8,128)(2,1)S(1)}, bf16[64,128]{1,0:T(8,128)(2,1)S(1)}) custom-call(f32[1]{0:T(128)S(6)} %copy.12.wave_ref, s32[8]{0:T(128)S(4)} %get-tuple-element.33.found_ref, bf16[32,640]{1,0:T(8,128)(2,1)S(1)} %collective-permute-done.3.data_ref.other_early, ...), custom_call_target="tpu_custom_call" | custom-call | flops 1 | bytes 1 | tf_op jit(solution)/shard_map/pallas_call | solution.py:464
  13.9 0.0 collective-permute-done.2.data_ref.own_ref.own_late
  13.9 0.3 %collective-permute-start.5 = (bf16[64,640]{1,0:T(8,128)(2,1)S(1)}, bf16[64,640]{1,0:T(8,128)(2,1)S(1)}, u32[]{:S(2)}, u32[]{:S(2)}) collective-permute-start(bf16[64,640]{1,0:T(8,128)(2,1)S(1)} %collective-permute-done.2.data_ref.own_ref.own_late), channel_id=1, source_target_pairs={{0,1},{1,0},{2,3},{3,2},{4,5},{5,4},{6,7},{7,6},{8,9},{9,8},{10,11... | collective-permute-start | bytes 245768 | tf_op jit(solution)/shard_map/ppermute | solution.py:490
  14.2 0.6 %shard_map.96 = (bf16[2,384,256]{2,1,0:T(8,128)(2,1)S(1)}, bf16[64,128]{1,0:T(8,128)(2,1)S(1)}, bf16[64,128]{1,0:T(8,128)(2,1)S(1)}) custom-call(f32[1]{0:T(128)S(6)} %copy.12.wave_ref, s32[8]{0:T(128)S(4)} %get-tuple-element.33.found_ref, bf16[64,640]{1,0:T(8,128)(2,1)S(1)} %collective-permute-done.2.data_ref.own_ref.own_late, ...), custom_call_target="tpu_custom_call" | custom-call | flops 1 | bytes 1 | tf_op jit(solution)/shard_map/pallas_call | solution.py:464
  14.8 0.5 %collective-permute-done.5.other_late = bf16[64,640]{1,0:T(8,128)(2,1)S(1)} collective-permute-done((bf16[64,640]{1,0:T(8,128)(2,1)S(1)}, bf16[64,640]{1,0:T(8,128)(2,1)S(1)}, u32[]{:S(2)}, u32[]{:S(2)}) %collective-permute-start.5) | collective-permute-done | bytes 81952 | tf_op jit(solution)/shard_map/ppermute | solution.py:490
  15.3 1.4 %shard_map.97 = f32[128,128]{1,0:T(8,128)} custom-call(f32[1]{0:T(128)S(6)} %copy.12.wave_ref, bf16[64,640]{1,0:T(8,128)(2,1)S(1)} %get-tuple-element.47.own_early, bf16[64,640]{1,0:T(8,128)(2,1)S(1)} %collective-permute-done.2.data_ref.own_ref.own_late, bf16[32,640]{1,0:T(8,128)(2,1)S(1)} %collective-permute-done.4.own_ref.other_first, ...), custom_call_target="tpu_custom_call" | custom-call | tf_op jit(solution)/shard_map/pallas_call | solution.py:523
  (4 shorter events, 0.0 us)
Async XLA Ops:
  1.2 4.2 %copy-start = (f32[6,256]{1,0:T(8,128)S(1)}, f32[6,256]{1,0:T(8,128)}, u32[]{:S(2)}) copy-start(f32[6,256]{1,0:T(8,128)} %tgeom_ref.11) | copy-start | bytes 18436
  1.2 5.1 %collective-permute-start = (bf16[16,640]{1,0:T(8,128)(2,1)S(1)}, bf16[16,640]{1,0:T(8,128)(2,1)S(1)}, u32[]{:S(2)}, u32[]{:S(2)}) collective-permute-start(bf16[16,640]{1,0:T(8,128)(2,1)S(1)} %get-tuple-element.34.data_ref.own_ref), channel_id=1, source_target_pairs={{0,9},{1,8},{2,11},{3,10},{4,13},{5,12},{6,15},{7,14},{8,1},{9,0},... | collective-permute-start | bytes 61448 | tf_op jit(solution)/shard_map/ppermute | solution.py:490
  6.3 3.5 %collective-permute-start.1 = (bf16[32,640]{1,0:T(8,128)(2,1)S(1)}, bf16[32,640]{1,0:T(8,128)(2,1)S(1)}, u32[]{:S(2)}, u32[]{:S(2)}) collective-permute-start(bf16[32,640]{1,0:T(8,128)(2,1)S(1)} %constant_dynamic-update-slice_fusion.own_ref), channel_id=1, source_target_pairs={{0,5},{1,2},{2,1},{3,6},{4,7},{5,0},{6,3},{7,4},{8,11},{9,12},{10,... | collective-permute-start | bytes 122888 | tf_op jit(solution)/shard_map/ppermute | solution.py:490
  9.8 4.1 %collective-permute-start.2 = (bf16[64,640]{1,0:T(8,128)(2,1)S(1)}, bf16[64,640]{1,0:T(8,128)(2,1)S(1)}, u32[]{:S(2)}, u32[]{:S(2)}) collective-permute-start(bf16[64,640]{1,0:T(8,128)(2,1)S(1)} %constant_dynamic-update-slice_fusion.2.own_ref), channel_id=1, source_target_pairs={{0,3},{1,4},{2,7},{3,0},{4,1},{5,6},{6,5},{7,2},{8,13},{9,10},{10,... | collective-permute-start | bytes 245768 | tf_op jit(solution)/shard_map/ppermute | solution.py:490
  11.5 1.3 %collective-permute-start.4 = (bf16[32,640]{1,0:T(8,128)(2,1)S(1)}, bf16[32,640]{1,0:T(8,128)(2,1)S(1)}, u32[]{:S(2)}, u32[]{:S(2)}) collective-permute-start(bf16[32,640]{1,0:T(8,128)(2,1)S(1)} %get-tuple-element.39), channel_id=1, source_target_pairs={{0,1},{1,0},{2,3},{3,2},{4,5},{5,4},{6,7},{7,6},{8,9},{9,8},{10,11... | collective-permute-start | bytes 122888 | tf_op jit(solution)/shard_map/ppermute | solution.py:490
  12.0 1.2 %collective-permute-start.3 = (bf16[32,640]{1,0:T(8,128)(2,1)S(1)}, bf16[32,640]{1,0:T(8,128)(2,1)S(1)}, u32[]{:S(2)}, u32[]{:S(2)}) collective-permute-start(bf16[32,640]{1,0:T(8,128)(2,1)S(1)} %collective-permute-done.1.data_ref), channel_id=1, source_target_pairs={{0,1},{1,0},{2,3},{3,2},{4,5},{5,4},{6,7},{7,6},{8,9},{9,8},{10,11... | collective-permute-start | bytes 122888 | tf_op jit(solution)/shard_map/ppermute | solution.py:490
  13.9 1.3 %collective-permute-start.5 = (bf16[64,640]{1,0:T(8,128)(2,1)S(1)}, bf16[64,640]{1,0:T(8,128)(2,1)S(1)}, u32[]{:S(2)}, u32[]{:S(2)}) collective-permute-start(bf16[64,640]{1,0:T(8,128)(2,1)S(1)} %collective-permute-done.2.data_ref.own_ref.own_late), channel_id=1, source_target_pairs={{0,1},{1,0},{2,3},{3,2},{4,5},{5,4},{6,7},{7,6},{8,9},{9,8},{10,11... | collective-permute-start | bytes 245768 | tf_op jit(solution)/shard_map/ppermute | solution.py:490
where the time goes:
time: 16.8 us; the launch traced here: 16.7 us
  starting transfers between devices  7.82 us (47%)
  Pallas kernels  5.19 us (31%)
  waiting for transfers between devices  2.86 us (17%)
  between operations  0.75 us (4%)
    ppermute x6, starting transfers between devices, moved(): return lax.ppermute(value, ('row', 'col'), pairs)  7.82 us
    ppermute x6, waiting for transfers between devices, moved(): return lax.ppermute(value, ('row', 'col'), pairs)  2.86 us
    pallas_call x5, Pallas kernels, near_blocks(): pl.pallas_call(functools.partial(near_kernel if first else first_near_ker...  2.66 us
    pallas_call x1, Pallas kernels, exchanged(): pl.pallas_call(functools.partial(last_kernel, exc, partner), out_shape=ja...  1.36 us
    pallas_call x1, Pallas kernels, packed(): pl.pallas_call(functools.partial(pack_kernel, units), out_shape=[pltpu.VM...  1.17 us
  transfers between devices with their start and end apart: 6, of which 5 were waited for; matrix products, arithmetic and copies ran while one was open for 0% of the time, Pallas kernels for 16%

commit v1 on v0

--- a/solution.py
+++ b/solution.py
@@ -394,13 +394,12 @@
             slot += 1
 
     late_kern = far_rows(other_late, exc, wave_ref[0], own_targets(tgeom_ref, rows))
-    other_kern = [
-        jnp.concatenate([early[...], x], 0)
-        for x, early in zip(late_kern, (early_re_ref, early_im_ref))
-    ]
+    first = other_first.shape[0]
     kern_re, kern_im = [
-        jnp.concatenate([ref[...] for ref in refs] + [last], 0).astype(F32)
-        for refs, last in zip((kern_re_refs, kern_im_refs), other_kern)
+        jnp.concatenate(
+            [*[ref[...] for ref in refs[:-2]], refs[-2][first:], refs[-1][...], refs[-2][:first], early[...], x], 0
+        ).astype(F32)
+        for refs, early, x in zip((kern_re_refs, kern_im_refs), (early_re_ref, early_im_ref), late_kern)
     ]
     excite = jnp.concatenate(
         [own[:, EXC_AT : EXC_AT + exc], other[:, EXC_AT : EXC_AT + exc]], 0
@@ -496,7 +495,11 @@
     for step, (a, b) in enumerate(steps):
         arriving = moved(own, a, b)
         slots = fresh.shape[0] // cpd
-        made = near_blocks(exc, done, slots, wavenumber, found, fresh, own, target, ut, tgt_geom, True)
+        last = step == len(steps) - 1
+        made = near_blocks(
+            exc, done, slots, wavenumber, found, fresh, other_first if last else own, target, ut, tgt_geom,
+            not last, last,
+        )
         near.extend(made[:3])
         if not done:
             ut = made[4]
@@ -504,13 +507,15 @@
             other_first = moved(made[3], 1, 1)
         done += slots
         fresh = arriving
-        if step < len(steps) - 1:
+        if not last:
             own = jnp.concatenate([made[3], arriving], 0)
+        if step == len(steps) - 2:
+            own, other_first = lax.optimization_barrier((own, other_first))
     half = own.shape[0] // 2
     other_early = moved(own[half:], 1, 1)
     quarter = half // cpd
     early = near_blocks(
-        exc, done, quarter, wavenumber, found, other_early, other_first, target, ut, tgt_geom, False, True
+        exc, done, quarter, wavenumber, found, other_early, other_early, target, ut, tgt_geom, False
     )
     fresh, early, made = lax.optimization_barrier((fresh, early, made))
     other_late = moved(fresh, 1, 1)
@@ -529,7 +534,7 @@
         compiler_params=SMALL,
     )(
         wavenumber,
-        *[in_vmem(x) for x in (made[3], fresh, other_first, other_early, other_late, tgt_geom, *early[1:], *near)],
+        *[in_vmem(x) for x in (own, fresh, other_first, other_early, other_late, tgt_geom, *early[1:], *near)],
     )
 
 

time: 16.8 us -> 16.8 us (level)
  starting transfers between devices: 7.82 us -> 8.37 us
  Pallas kernels: 5.19 us -> 4.83 us
  waiting for transfers between devices: 2.86 us -> 2.6 us
    ppermute x6, starting transfers between devices: 7.82 us -> 8.37 us  [moved(): return lax.ppermute(value, ('row', 'col'), pairs)]
    pallas_call x5, Pallas kernels: 2.66 us -> 2.29 us  [near_blocks(): pl.pallas_call(functools.partial(near_kernel if first else first_near_ker...]
    ppermute x6, waiting for transfers between devices: 2.86 us -> 2.6 us  [moved(): return lax.ppermute(value, ('row', 'col'), pairs)]
  transfers between devices with their start and end apart: 6 -> 6, of which waited for: 5 -> 6; matrix products, arithmetic and copies ran while one was open for 0% -> 0% of each run, Pallas kernels for 16% -> 14%
where the time goes in v1:
time: 16.8 us; the launch traced here: 16.6 us
  starting transfers between devices  8.37 us (50%)
  Pallas kernels  4.83 us (29%)
  waiting for transfers between devices  2.6 us (15%)
  between operations  0.73 us (4%)
    ppermute x6, starting transfers between devices, moved(): return lax.ppermute(value, ('row', 'col'), pairs)  8.37 us
    ppermute x6, waiting for transfers between devices, moved(): return lax.ppermute(value, ('row', 'col'), pairs)  2.6 us
    pallas_call x5, Pallas kernels, near_blocks(): pl.pallas_call(functools.partial(near_kernel if first else first_near_ker...  2.29 us
    pallas_call x1, Pallas kernels, exchanged(): pl.pallas_call(functools.partial(last_kernel, exc, partner), out_shape=ja...  1.36 us
    pallas_call x1, Pallas kernels, packed(): pl.pallas_call(functools.partial(pack_kernel, units), out_shape=[pltpu.VM...  1.17 us
  transfers between devices with their start and end apart: 6, of which 6 were waited for; matrix products, arithmetic and copies ran while one was open for 0% of the time, Pallas kernels for 14%

profile of v1, /device:TPU:0, one launch (start us, length us, event | category | flops | bytes accessed | tf_op | source)
XLA Modules:
  0.0 16.6 jit_solution(11351399229264082670)
XLA Ops:
  0.0 1.2 %shard_map.91 = (bf16[16,640]{1,0:T(8,128)(2,1)S(1)}, f32[3,8,128]{2,1,0:T(8,128)S(1)}, bf16[2,192,128]{2,1,0:T(8,128)(2,1)S(1)}, s32[8]{0:T(128)S(4)}) custom-call(s32[2,9]{1,0:T(2,128)} %order_hbm.1, f32[4,16]{1,0:T(4,128)} %geom_hbm.1, bf16[16,128]{1,0:T(8,128)(2,1)} %bitcast.3, f32[3,192]{1,0:T(4,128)} %nodes_hbm.1, bf16[2,16,192]{2,1,0:T(8,128)(2,1)} %bitcast.2, ...), custom_call_target="tpu_custom_call" | custom-call | tf_op jit(solution)/shard_map/pallas_call | solution.py:439
  1.2 0.0 copy-start
  1.2 3.5 %collective-permute-start = (bf16[16,640]{1,0:T(8,128)(2,1)S(1)}, bf16[16,640]{1,0:T(8,128)(2,1)S(1)}, u32[]{:S(2)}, u32[]{:S(2)}) collective-permute-start(bf16[16,640]{1,0:T(8,128)(2,1)S(1)} %get-tuple-element.34.data_ref.own_ref), channel_id=1, source_target_pairs={{0,9},{1,8},{2,11},{3,10},{4,13},{5,12},{6,15},{7,14},{8,1},{9,0},... | collective-permute-start | bytes 61448 | tf_op jit(solution)/shard_map/ppermute | solution.py:489
  5.4 0.0 copy-done
  5.4 0.2 %shard_map.92 = (bf16[1,384,256]{2,1,0:T(8,128)(2,1)S(1)}, bf16[16,128]{1,0:T(8,128)(2,1)S(1)}, bf16[16,128]{1,0:T(8,128)(2,1)S(1)}, bf16[16,640]{1,0:T(8,128)(2,1)S(1)}, bf16[384,256]{1,0:T(8,128)(2,1)S(1)}) custom-call(f32[1]{0:T(128)S(6)} %copy.11.wave_ref, s32[8]{0:T(128)S(4)} %get-tuple-element.33.found_ref, ...), custom_call_target="tpu_custom_call" | custom-call | flops 1 | bytes 1 | tf_op jit(solution)/shard_map/pallas_call | solution.py:463
  5.6 0.6 %collective-permute-done.data_ref = bf16[16,640]{1,0:T(8,128)(2,1)S(1)} collective-permute-done((bf16[16,640]{1,0:T(8,128)(2,1)S(1)}, bf16[16,640]{1,0:T(8,128)(2,1)S(1)}, u32[]{:S(2)}, u32[]{:S(2)}) %collective-permute-start) | collective-permute-done | bytes 20512 | tf_op jit(solution)/shard_map/ppermute | solution.py:489
  6.3 1.9 %collective-permute-start.1 = (bf16[32,640]{1,0:T(8,128)(2,1)S(1)}, bf16[32,640]{1,0:T(8,128)(2,1)S(1)}, u32[]{:S(2)}, u32[]{:S(2)}) collective-permute-start(bf16[32,640]{1,0:T(8,128)(2,1)S(1)} %constant_dynamic-update-slice_fusion.own_ref), channel_id=1, source_target_pairs={{0,5},{1,2},{2,1},{3,6},{4,7},{5,0},{6,3},{7,4},{8,11},{9,12},{10,... | collective-permute-start | bytes 122888 | tf_op jit(solution)/shard_map/ppermute | solution.py:489
  8.1 0.5 %shard_map.93 = (bf16[1,384,256]{2,1,0:T(8,128)(2,1)S(1)}, bf16[16,128]{1,0:T(8,128)(2,1)S(1)}, bf16[16,128]{1,0:T(8,128)(2,1)S(1)}, bf16[32,640]{1,0:T(8,128)(2,1)S(1)}) custom-call(f32[1]{0:T(128)S(6)} %copy.11.wave_ref, s32[8]{0:T(128)S(4)} %get-tuple-element.33.found_ref, bf16[16,640]{1,0:T(8,128)(2,1)S(1)} %collective-permute-done.data_ref, ...), custom_call_target="tpu_custom_call" | custom-call | flops 1 | bytes 1 | tf_op jit(solution)/shard_map/pallas_call | solution.py:463
  8.6 0.3 %collective-permute-start.2 = (bf16[32,640]{1,0:T(8,128)(2,1)S(1)}, bf16[32,640]{1,0:T(8,128)(2,1)S(1)}, u32[]{:S(2)}, u32[]{:S(2)}) collective-permute-start(bf16[32,640]{1,0:T(8,128)(2,1)S(1)} %get-tuple-element.39), channel_id=1, source_target_pairs={{0,1},{1,0},{2,3},{3,2},{4,5},{5,4},{6,7},{7,6},{8,9},{9,8},{10,11... | collective-permute-start | bytes 122888 | tf_op jit(solution)/shard_map/ppermute | solution.py:489
  8.9 0.9 %collective-permute-done.1.data_ref = bf16[32,640]{1,0:T(8,128)(2,1)S(1)} collective-permute-done((bf16[32,640]{1,0:T(8,128)(2,1)S(1)}, bf16[32,640]{1,0:T(8,128)(2,1)S(1)}, u32[]{:S(2)}, u32[]{:S(2)}) %collective-permute-start.1) | collective-permute-done | bytes 40992 | tf_op jit(solution)/shard_map/ppermute | solution.py:489
  9.8 0.1 collective-permute-done.2.own_ref.other_first
  9.9 1.7 %collective-permute-start.3 = (bf16[64,640]{1,0:T(8,128)(2,1)S(1)}, bf16[64,640]{1,0:T(8,128)(2,1)S(1)}, u32[]{:S(2)}, u32[]{:S(2)}) collective-permute-start(bf16[64,640]{1,0:T(8,128)(2,1)S(1)} %pad_maximum_fusion.own_early), channel_id=1, source_target_pairs={{0,3},{1,4},{2,7},{3,0},{4,1},{5,6},{6,5},{7,2},{8,13},{9,10},{10,... | collective-permute-start | bytes 245768 | tf_op jit(solution)/shard_map/ppermute | solution.py:489
  11.6 0.5 %collective-permute-start.4 = (bf16[32,640]{1,0:T(8,128)(2,1)S(1)}, bf16[32,640]{1,0:T(8,128)(2,1)S(1)}, u32[]{:S(2)}, u32[]{:S(2)}) collective-permute-start(bf16[32,640]{1,0:T(8,128)(2,1)S(1)} %slice.3), channel_id=1, source_target_pairs={{0,1},{1,0},{2,3},{3,2},{4,5},{5,4},{6,7},{7,6},{8,9},{9,8},{10,11... | collective-permute-start | bytes 122888 | tf_op jit(solution)/shard_map/ppermute | solution.py:489
  12.0 0.6 %shard_map.95 = (bf16[2,384,256]{2,1,0:T(8,128)(2,1)S(1)}, bf16[64,128]{1,0:T(8,128)(2,1)S(1)}, bf16[64,128]{1,0:T(8,128)(2,1)S(1)}) custom-call(f32[1]{0:T(128)S(6)} %copy.11.wave_ref, s32[8]{0:T(128)S(4)} %get-tuple-element.33.found_ref, bf16[32,640]{1,0:T(8,128)(2,1)S(1)} %collective-permute-done.1.data_ref, ...), custom_call_target="tpu_custom_call" | custom-call | flops 1 | bytes 1 | tf_op jit(solution)/shard_map/pallas_call | solution.py:463
  12.6 0.3 %collective-permute-done.4.data_ref.own_ref.other_early = bf16[32,640]{1,0:T(8,128)(2,1)S(1)} collective-permute-done((bf16[32,640]{1,0:T(8,128)(2,1)S(1)}, bf16[32,640]{1,0:T(8,128)(2,1)S(1)}, u32[]{:S(2)}, u32[]{:S(2)}) %collective-permute-start.4) | collective-permute-done | bytes 40992 | tf_op jit(solution)/shard_map/ppermute | solution.py:489
  12.9 0.5 %shard_map.94 = (bf16[2,384,256]{2,1,0:T(8,128)(2,1)S(1)}, bf16[32,128]{1,0:T(8,128)(2,1)S(1)}, bf16[32,128]{1,0:T(8,128)(2,1)S(1)}) custom-call(f32[1]{0:T(128)S(6)} %copy.11.wave_ref, s32[8]{0:T(128)S(4)} %get-tuple-element.33.found_ref, bf16[32,640]{1,0:T(8,128)(2,1)S(1)} %collective-permute-done.4.data_ref.own_ref.other_early, ...), custom_call_target="tpu_custom_call" | custom-call | flops 1 | bytes 1 | tf_op jit(solution)/shard_map/pallas_call | solution.py:463
  13.4 0.4 %collective-permute-done.3.data_ref.own_ref.own_late = bf16[64,640]{1,0:T(8,128)(2,1)S(1)} collective-permute-done((bf16[64,640]{1,0:T(8,128)(2,1)S(1)}, bf16[64,640]{1,0:T(8,128)(2,1)S(1)}, u32[]{:S(2)}, u32[]{:S(2)}) %collective-permute-start.3) | collective-permute-done | bytes 81952 | tf_op jit(solution)/shard_map/ppermute | solution.py:489
  13.8 0.5 %collective-permute-start.5 = (bf16[64,640]{1,0:T(8,128)(2,1)S(1)}, bf16[64,640]{1,0:T(8,128)(2,1)S(1)}, u32[]{:S(2)}, u32[]{:S(2)}) collective-permute-start(bf16[64,640]{1,0:T(8,128)(2,1)S(1)} %collective-permute-done.3.data_ref.own_ref.own_late), channel_id=1, source_target_pairs={{0,1},{1,0},{2,3},{3,2},{4,5},{5,4},{6,7},{7,6},{8,9},{9,8},{10,11... | collective-permute-start | bytes 245768 | tf_op jit(solution)/shard_map/ppermute | solution.py:489
  14.3 0.6 %shard_map.96 = (bf16[2,384,256]{2,1,0:T(8,128)(2,1)S(1)}, bf16[64,128]{1,0:T(8,128)(2,1)S(1)}, bf16[64,128]{1,0:T(8,128)(2,1)S(1)}) custom-call(f32[1]{0:T(128)S(6)} %copy.11.wave_ref, s32[8]{0:T(128)S(4)} %get-tuple-element.33.found_ref, bf16[64,640]{1,0:T(8,128)(2,1)S(1)} %collective-permute-done.3.data_ref.own_ref.own_late, ...), custom_call_target="tpu_custom_call" | custom-call | flops 1 | bytes 1 | tf_op jit(solution)/shard_map/pallas_call | solution.py:463
  14.8 0.4 %collective-permute-done.5.other_late = bf16[64,640]{1,0:T(8,128)(2,1)S(1)} collective-permute-done((bf16[64,640]{1,0:T(8,128)(2,1)S(1)}, bf16[64,640]{1,0:T(8,128)(2,1)S(1)}, u32[]{:S(2)}, u32[]{:S(2)}) %collective-permute-start.5) | collective-permute-done | bytes 81952 | tf_op jit(solution)/shard_map/ppermute | solution.py:489
  15.2 1.4 %shard_map.97 = f32[128,128]{1,0:T(8,128)} custom-call(f32[1]{0:T(128)S(6)} %copy.11.wave_ref, bf16[64,640]{1,0:T(8,128)(2,1)S(1)} %pad_maximum_fusion.own_early, bf16[64,640]{1,0:T(8,128)(2,1)S(1)} %collective-permute-done.3.data_ref.own_ref.own_late, bf16[32,640]{1,0:T(8,128)(2,1)S(1)} %collective-permute-done.2.own_ref.other_first, ...), custom_call_target="tpu_custom_call" | custom-call | tf_op jit(solution)/shard_map/pallas_call | solution.py:528
  (4 shorter events, 0.0 us)
Async XLA Ops:
  1.2 4.2 %copy-start = (f32[6,256]{1,0:T(8,128)S(1)}, f32[6,256]{1,0:T(8,128)}, u32[]{:S(2)}) copy-start(f32[6,256]{1,0:T(8,128)} %tgeom_ref.11) | copy-start | bytes 18436
  1.2 5.1 %collective-permute-start = (bf16[16,640]{1,0:T(8,128)(2,1)S(1)}, bf16[16,640]{1,0:T(8,128)(2,1)S(1)}, u32[]{:S(2)}, u32[]{:S(2)}) collective-permute-start(bf16[16,640]{1,0:T(8,128)(2,1)S(1)} %get-tuple-element.34.data_ref.own_ref), channel_id=1, source_target_pairs={{0,9},{1,8},{2,11},{3,10},{4,13},{5,12},{6,15},{7,14},{8,1},{9,0},... | collective-permute-start | bytes 61448 | tf_op jit(solution)/shard_map/ppermute | solution.py:489
  6.3 3.5 %collective-permute-start.1 = (bf16[32,640]{1,0:T(8,128)(2,1)S(1)}, bf16[32,640]{1,0:T(8,128)(2,1)S(1)}, u32[]{:S(2)}, u32[]{:S(2)}) collective-permute-start(bf16[32,640]{1,0:T(8,128)(2,1)S(1)} %constant_dynamic-update-slice_fusion.own_ref), channel_id=1, source_target_pairs={{0,5},{1,2},{2,1},{3,6},{4,7},{5,0},{6,3},{7,4},{8,11},{9,12},{10,... | collective-permute-start | bytes 122888 | tf_op jit(solution)/shard_map/ppermute | solution.py:489
  8.6 1.3 %collective-permute-start.2 = (bf16[32,640]{1,0:T(8,128)(2,1)S(1)}, bf16[32,640]{1,0:T(8,128)(2,1)S(1)}, u32[]{:S(2)}, u32[]{:S(2)}) collective-permute-start(bf16[32,640]{1,0:T(8,128)(2,1)S(1)} %get-tuple-element.39), channel_id=1, source_target_pairs={{0,1},{1,0},{2,3},{3,2},{4,5},{5,4},{6,7},{7,6},{8,9},{9,8},{10,11... | collective-permute-start | bytes 122888 | tf_op jit(solution)/shard_map/ppermute | solution.py:489
  9.9 3.9 %collective-permute-start.3 = (bf16[64,640]{1,0:T(8,128)(2,1)S(1)}, bf16[64,640]{1,0:T(8,128)(2,1)S(1)}, u32[]{:S(2)}, u32[]{:S(2)}) collective-permute-start(bf16[64,640]{1,0:T(8,128)(2,1)S(1)} %pad_maximum_fusion.own_early), channel_id=1, source_target_pairs={{0,3},{1,4},{2,7},{3,0},{4,1},{5,6},{6,5},{7,2},{8,13},{9,10},{10,... | collective-permute-start | bytes 245768 | tf_op jit(solution)/shard_map/ppermute | solution.py:489
  11.6 1.3 %collective-permute-start.4 = (bf16[32,640]{1,0:T(8,128)(2,1)S(1)}, bf16[32,640]{1,0:T(8,128)(2,1)S(1)}, u32[]{:S(2)}, u32[]{:S(2)}) collective-permute-start(bf16[32,640]{1,0:T(8,128)(2,1)S(1)} %slice.3), channel_id=1, source_target_pairs={{0,1},{1,0},{2,3},{3,2},{4,5},{5,4},{6,7},{7,6},{8,9},{9,8},{10,11... | collective-permute-start | bytes 122888 | tf_op jit(solution)/shard_map/ppermute | solution.py:489
  13.8 1.4 %collective-permute-start.5 = (bf16[64,640]{1,0:T(8,128)(2,1)S(1)}, bf16[64,640]{1,0:T(8,128)(2,1)S(1)}, u32[]{:S(2)}, u32[]{:S(2)}) collective-permute-start(bf16[64,640]{1,0:T(8,128)(2,1)S(1)} %collective-permute-done.3.data_ref.own_ref.own_late), channel_id=1, source_target_pairs={{0,1},{1,0},{2,3},{3,2},{4,5},{5,4},{6,7},{7,6},{8,9},{9,8},{10,11... | collective-permute-start | bytes 245768 | tf_op jit(solution)/shard_map/ppermute | solution.py:489

commit v2 on v1

--- a/solution.py
+++ b/solution.py
@@ -355,9 +355,37 @@
     near_kernel(exc, first, wave_ref, found_ref, data_ref, own_ref, target_ref, ut_ref, tgeom_ref, *refs)
 
 
+def weight_rows(data):
+    sign = jnp.where(iota((1, LANES), 1) < QSTEP, 1.0, -1.0).astype(BF16)
+    w = [data[:, i * LANES : (i + 1) * LANES] for i in range(3)]
+    swapped = jnp.concatenate([w[2][:, QSTEP:], w[2][:, :QSTEP]], 1)
+    return jnp.concatenate([w[0], -w[1], w[2] * sign], 1), jnp.concatenate([w[1], w[0], swapped], 1)
+
+
+def near_rows(left, v):
+    product = dot(left, v)
+    return (product[:, :LANES] + product[:, LANES:]) * INV_FOUR_PI
+
+
+def known_kernel(own_ref, fresh_ref, other_first, other_early, *refs):
+    *v_refs, out_ref = refs
+    cpd = 16
+    pairs = [(own_ref, other_first), (fresh_ref, other_early)]
+    v = [ref[i] for ref in v_refs for i in range(ref.shape[0])]
+    rows = []
+    for own_half, other_half in pairs:
+        other_re, other_im = weight_rows(other_half[...])
+        own_re, own_im = weight_rows(own_half[: other_half.shape[0]])
+        for k in range(other_half.shape[0] // cpd):
+            here = slice(k * cpd, (k + 1) * cpd)
+            rows.append(jnp.concatenate([own_re[here], other_re[here], own_im[here], other_im[here]], 0))
+    for k, left in enumerate(rows):
+        out_ref[k] = near_rows(left, v[k])
+
+
 def last_kernel(
     exc, partner, wave_ref, own_early, own_late, other_first, other_early, other_late, tgeom_ref,
-    early_re_ref, early_im_ref, *refs
+    known_ref, early_re_ref, early_im_ref, *refs
 ):
     own = jnp.concatenate([own_early[...], own_late[...]], 0)
     other = jnp.concatenate([other_first[...], other_early[...], other_late[...]], 0)
@@ -369,13 +397,8 @@
     cpd = 16
     main = LANES
     slots = len(partner)
-    sign = jnp.where(lax.broadcasted_iota(jnp.int32, (1, LANES), 1) < QSTEP, 1.0, -1.0).astype(BF16)
-
-    def weight_rows(data):
-        w = [data[:, i * main : (i + 1) * main] for i in range(3)]
-        swapped = jnp.concatenate([w[2][:, QSTEP:], w[2][:, :QSTEP]], 1)
-        return jnp.concatenate([w[0], -w[1], w[2] * sign], 1), jnp.concatenate([w[1], w[0], swapped], 1)
-
+    quarter = slots // 4
+    known = [*range(quarter), *range(2 * quarter, 3 * quarter)]
     own_re, own_im = weight_rows(own)
     other_re, other_im = weight_rows(other)
     slot = 0
@@ -383,9 +406,11 @@
         for i in range(v_ref.shape[0]):
             here = slice(slot * cpd, (slot + 1) * cpd)
             there = slice(partner[slot] * cpd, (partner[slot] + 1) * cpd)
-            left = jnp.concatenate([own_re[here], other_re[there], own_im[here], other_im[there]], 0)
-            product = dot(left, v_ref[i])
-            a = (product[:, :LANES] + product[:, LANES:]) * INV_FOUR_PI
+            if slot in known:
+                a = known_ref[known.index(slot)]
+            else:
+                left = jnp.concatenate([own_re[here], other_re[there], own_im[here], other_im[there]], 0)
+                a = near_rows(left, v_ref[i])
             there = slice((slots + partner[slot]) * cpd, (slots + partner[slot] + 1) * cpd)
             zre[here] = a[0:cpd]
             zre[there] = a[cpd : 2 * cpd]
@@ -524,17 +549,26 @@
     )
     near.append(early[0])
     near.extend(late)
+    firsts = [v for v in near[: 3 * (len(steps) - 1) : 3]]
+    known = pl.pallas_call(
+        known_kernel,
+        out_shape=pltpu.VMEM((2 * quarter, 4 * cpd, rows_here), F32),
+        in_specs=[VMEM_SPEC] * (5 + len(firsts)),
+        out_specs=VMEM_SPEC,
+        compiler_params=SMALL,
+        cost_estimate=pl.CostEstimate(flops=1, bytes_accessed=1, transcendentals=0),
+    )(*[in_vmem(x) for x in (own, fresh, other_first, other_early, *firsts, early[0])])
     partner = [units[1].index(u) for u in units[0]]
     return pl.pallas_call(
         functools.partial(last_kernel, exc, partner),
         out_shape=jax.ShapeDtypeStruct((rows_here, exc), F32),
-        in_specs=[SMEM_SPEC] + [VMEM_SPEC] * (8 + len(near)),
+        in_specs=[SMEM_SPEC] + [VMEM_SPEC] * (9 + len(near)),
         out_specs=VMEM_SPEC,
         scratch_shapes=[pltpu.VMEM((count * cpd, rows_here), F32)] * 2,
         compiler_params=SMALL,
     )(
         wavenumber,
-        *[in_vmem(x) for x in (own, fresh, other_first, other_early, other_late, tgt_geom, *early[1:], *near)],
+        *[in_vmem(x) for x in (own, fresh, other_first, other_early, other_late, tgt_geom, known, *early[1:], *near)],
     )
 
 

time: 16.8 us -> 16.7 us (level)
  starting transfers between devices: 8.37 us -> 7.74 us
  Pallas kernels: 4.83 us -> 5.08 us
  waiting for transfers between devices: 2.6 us -> 2.85 us
    ppermute x6, starting transfers between devices: 8.37 us -> 7.74 us  [moved(): return lax.ppermute(value, ('row', 'col'), pairs)]
    ppermute x6, waiting for transfers between devices: 2.6 us -> 2.85 us  [moved(): return lax.ppermute(value, ('row', 'col'), pairs)]
    pallas_call x0 -> x1, Pallas kernels: none -> 0.25 us  [exchanged(): pl.pallas_call(known_kernel, out_shape=pltpu.VMEM((2 * quarter, 4 * cpd,...]
  transfers between devices with their start and end apart: 6 -> 6, of which waited for: 6 -> 6; matrix products, arithmetic and copies ran while one was open for 0% -> 0% of each run, Pallas kernels for 14% -> 16%
where the time goes in v2:
time: 16.7 us; the launch traced here: 16.5 us
  starting transfers between devices  7.74 us (46%)
  Pallas kernels  5.08 us (30%)
  waiting for transfers between devices  2.85 us (17%)
  between operations  0.75 us (4%)
    ppermute x6, starting transfers between devices, moved(): return lax.ppermute(value, ('row', 'col'), pairs)  7.74 us
    ppermute x6, waiting for transfers between devices, moved(): return lax.ppermute(value, ('row', 'col'), pairs)  2.85 us
    pallas_call x5, Pallas kernels, near_blocks(): pl.pallas_call(functools.partial(near_kernel if first else first_near_ker...  2.42 us
    pallas_call x1, Pallas kernels, exchanged(): pl.pallas_call(functools.partial(last_kernel, exc, partner), out_shape=ja...  1.23 us
    pallas_call x1, Pallas kernels, packed(): pl.pallas_call(functools.partial(pack_kernel, units), out_shape=[pltpu.VM...  1.17 us
  transfers between devices with their start and end apart: 6, of which 6 were waited for; matrix products, arithmetic and copies ran while one was open for 0% of the time, Pallas kernels for 16%

profile of v2, /device:TPU:0, one launch (start us, length us, event | category | flops | bytes accessed | tf_op | source)
XLA Modules:
  0.0 16.5 jit_solution(16040292235630036001)
XLA Ops:
  0.0 1.2 %shard_map.91 = (bf16[16,640]{1,0:T(8,128)(2,1)S(1)}, f32[3,8,128]{2,1,0:T(8,128)S(1)}, bf16[2,192,128]{2,1,0:T(8,128)(2,1)S(1)}, s32[8]{0:T(128)S(4)}) custom-call(s32[2,9]{1,0:T(2,128)} %order_hbm.1, f32[4,16]{1,0:T(4,128)} %geom_hbm.1, bf16[16,128]{1,0:T(8,128)(2,1)} %bitcast.3, f32[3,192]{1,0:T(4,128)} %nodes_hbm.1, bf16[2,16,192]{2,1,0:T(8,128)(2,1)} %bitcast.2, ...), custom_call_target="tpu_custom_call" | custom-call | tf_op jit(solution)/shard_map/pallas_call | solution.py:464
  1.2 0.0 copy-start
  1.2 3.5 %collective-permute-start = (bf16[16,640]{1,0:T(8,128)(2,1)S(1)}, bf16[16,640]{1,0:T(8,128)(2,1)S(1)}, u32[]{:S(2)}, u32[]{:S(2)}) collective-permute-start(bf16[16,640]{1,0:T(8,128)(2,1)S(1)} %get-tuple-element.34.data_ref.own_ref), channel_id=1, source_target_pairs={{0,9},{1,8},{2,11},{3,10},{4,13},{5,12},{6,15},{7,14},{8,1},{9,0},... | collective-permute-start | bytes 61448 | tf_op jit(solution)/shard_map/ppermute | solution.py:514
  5.4 0.0 copy-done
  5.4 0.4 %shard_map.92 = (bf16[1,384,256]{2,1,0:T(8,128)(2,1)S(1)}, bf16[16,128]{1,0:T(8,128)(2,1)S(1)}, bf16[16,128]{1,0:T(8,128)(2,1)S(1)}, bf16[16,640]{1,0:T(8,128)(2,1)S(1)}, bf16[384,256]{1,0:T(8,128)(2,1)S(1)}) custom-call(f32[1]{0:T(128)S(6)} %copy.11.wave_ref, s32[8]{0:T(128)S(4)} %get-tuple-element.33.found_ref, ...), custom_call_target="tpu_custom_call" | custom-call | flops 1 | bytes 1 | tf_op jit(solution)/shard_map/pallas_call | solution.py:488
  5.9 0.4 %collective-permute-done.data_ref = bf16[16,640]{1,0:T(8,128)(2,1)S(1)} collective-permute-done((bf16[16,640]{1,0:T(8,128)(2,1)S(1)}, bf16[16,640]{1,0:T(8,128)(2,1)S(1)}, u32[]{:S(2)}, u32[]{:S(2)}) %collective-permute-start) | collective-permute-done | bytes 20512 | tf_op jit(solution)/shard_map/ppermute | solution.py:514
  6.3 1.9 %collective-permute-start.1 = (bf16[32,640]{1,0:T(8,128)(2,1)S(1)}, bf16[32,640]{1,0:T(8,128)(2,1)S(1)}, u32[]{:S(2)}, u32[]{:S(2)}) collective-permute-start(bf16[32,640]{1,0:T(8,128)(2,1)S(1)} %constant_dynamic-update-slice_fusion.own_ref), channel_id=1, source_target_pairs={{0,5},{1,2},{2,1},{3,6},{4,7},{5,0},{6,3},{7,4},{8,11},{9,12},{10,... | collective-permute-start | bytes 122888 | tf_op jit(solution)/shard_map/ppermute | solution.py:514
  8.1 0.7 %shard_map.93 = (bf16[1,384,256]{2,1,0:T(8,128)(2,1)S(1)}, bf16[16,128]{1,0:T(8,128)(2,1)S(1)}, bf16[16,128]{1,0:T(8,128)(2,1)S(1)}, bf16[32,640]{1,0:T(8,128)(2,1)S(1)}) custom-call(f32[1]{0:T(128)S(6)} %copy.11.wave_ref, s32[8]{0:T(128)S(4)} %get-tuple-element.33.found_ref, bf16[16,640]{1,0:T(8,128)(2,1)S(1)} %collective-permute-done.data_ref, ...), custom_call_target="tpu_custom_call" | custom-call | flops 1 | bytes 1 | tf_op jit(solution)/shard_map/pallas_call | solution.py:488
  8.8 0.1 collective-permute-start.2
  8.9 0.9 %collective-permute-done.1.data_ref = bf16[32,640]{1,0:T(8,128)(2,1)S(1)} collective-permute-done((bf16[32,640]{1,0:T(8,128)(2,1)S(1)}, bf16[32,640]{1,0:T(8,128)(2,1)S(1)}, u32[]{:S(2)}, u32[]{:S(2)}) %collective-permute-start.1) | collective-permute-done | bytes 40992 | tf_op jit(solution)/shard_map/ppermute | solution.py:514
  9.8 0.3 %collective-permute-done.2.own_ref.other_first = bf16[32,640]{1,0:T(8,128)(2,1)S(1)} collective-permute-done((bf16[32,640]{1,0:T(8,128)(2,1)S(1)}, bf16[32,640]{1,0:T(8,128)(2,1)S(1)}, u32[]{:S(2)}, u32[]{:S(2)}) %collective-permute-start.2) | collective-permute-done | bytes 40992 | tf_op jit(solution)/shard_map/ppermute | solution.py:514
  10.1 1.5 %collective-permute-start.3 = (bf16[64,640]{1,0:T(8,128)(2,1)S(1)}, bf16[64,640]{1,0:T(8,128)(2,1)S(1)}, u32[]{:S(2)}, u32[]{:S(2)}) collective-permute-start(bf16[64,640]{1,0:T(8,128)(2,1)S(1)} %pad_maximum_fusion.own_ref.own_early), channel_id=1, source_target_pairs={{0,3},{1,4},{2,7},{3,0},{4,1},{5,6},{6,5},{7,2},{8,13},{9,10},{10,... | collective-permute-start | bytes 245768 | tf_op jit(solution)/shard_map/ppermute | solution.py:514
  11.6 0.5 %collective-permute-start.4 = (bf16[32,640]{1,0:T(8,128)(2,1)S(1)}, bf16[32,640]{1,0:T(8,128)(2,1)S(1)}, u32[]{:S(2)}, u32[]{:S(2)}) collective-permute-start(bf16[32,640]{1,0:T(8,128)(2,1)S(1)} %slice.3), channel_id=1, source_target_pairs={{0,1},{1,0},{2,3},{3,2},{4,5},{5,4},{6,7},{7,6},{8,9},{9,8},{10,11... | collective-permute-start | bytes 122888 | tf_op jit(solution)/shard_map/ppermute | solution.py:514
  12.0 0.3 %shard_map.95 = (bf16[2,384,256]{2,1,0:T(8,128)(2,1)S(1)}, bf16[64,128]{1,0:T(8,128)(2,1)S(1)}, bf16[64,128]{1,0:T(8,128)(2,1)S(1)}) custom-call(f32[1]{0:T(128)S(6)} %copy.11.wave_ref, s32[8]{0:T(128)S(4)} %get-tuple-element.33.found_ref, bf16[32,640]{1,0:T(8,128)(2,1)S(1)} %collective-permute-done.1.data_ref, ...), custom_call_target="tpu_custom_call" | custom-call | flops 1 | bytes 1 | tf_op jit(solution)/shard_map/pallas_call | solution.py:488
  12.3 0.6 %collective-permute-done.4.data_ref.own_ref.other_early = bf16[32,640]{1,0:T(8,128)(2,1)S(1)} collective-permute-done((bf16[32,640]{1,0:T(8,128)(2,1)S(1)}, bf16[32,640]{1,0:T(8,128)(2,1)S(1)}, u32[]{:S(2)}, u32[]{:S(2)}) %collective-permute-start.4) | collective-permute-done | bytes 40992 | tf_op jit(solution)/shard_map/ppermute | solution.py:514
  12.9 0.5 %shard_map.94 = (bf16[2,384,256]{2,1,0:T(8,128)(2,1)S(1)}, bf16[32,128]{1,0:T(8,128)(2,1)S(1)}, bf16[32,128]{1,0:T(8,128)(2,1)S(1)}) custom-call(f32[1]{0:T(128)S(6)} %copy.11.wave_ref, s32[8]{0:T(128)S(4)} %get-tuple-element.33.found_ref, bf16[32,640]{1,0:T(8,128)(2,1)S(1)} %collective-permute-done.4.data_ref.own_ref.other_early, ...), custom_call_target="tpu_custom_call" | custom-call | flops 1 | bytes 1 | tf_op jit(solution)/shard_map/pallas_call | solution.py:488
  13.4 0.5 %collective-permute-done.3.fresh_ref.data_ref.own_ref.own_late = bf16[64,640]{1,0:T(8,128)(2,1)S(1)} collective-permute-done((bf16[64,640]{1,0:T(8,128)(2,1)S(1)}, bf16[64,640]{1,0:T(8,128)(2,1)S(1)}, u32[]{:S(2)}, u32[]{:S(2)}) %collective-permute-start.3) | collective-permute-done | bytes 81952 | tf_op jit(solution)/shard_map/ppermute | solution.py:514
  13.9 0.3 %collective-permute-start.5 = (bf16[64,640]{1,0:T(8,128)(2,1)S(1)}, bf16[64,640]{1,0:T(8,128)(2,1)S(1)}, u32[]{:S(2)}, u32[]{:S(2)}) collective-permute-start(bf16[64,640]{1,0:T(8,128)(2,1)S(1)} %collective-permute-done.3.fresh_ref.data_ref.own_ref.own_late), channel_id=1, source_target_pairs={{0,1},{1,0},{2,3},{3,2},{4,5},{5,4},{6,7},{7,6},{8,9},{9,8},{10,11... | collective-permute-start | bytes 245768 | tf_op jit(solution)/shard_map/ppermute | solution.py:514
  14.3 0.5 %shard_map.97 = (bf16[2,384,256]{2,1,0:T(8,128)(2,1)S(1)}, bf16[64,128]{1,0:T(8,128)(2,1)S(1)}, bf16[64,128]{1,0:T(8,128)(2,1)S(1)}) custom-call(f32[1]{0:T(128)S(6)} %copy.11.wave_ref, s32[8]{0:T(128)S(4)} %get-tuple-element.33.found_ref, bf16[64,640]{1,0:T(8,128)(2,1)S(1)} %collective-permute-done.3.fresh_ref.data_ref.own_ref.own_late, ...), custom_call_target="tpu_custom_call" | custom-call | flops 1 | bytes 1 | tf_op jit(solution)/shard_map/pallas_call | solution.py:488
  14.8 0.3 %shard_map.96.known_ref = f32[4,64,128]{2,1,0:T(8,128)S(1)} custom-call(bf16[64,640]{1,0:T(8,128)(2,1)S(1)} %pad_maximum_fusion.own_ref.own_early, bf16[64,640]{1,0:T(8,128)(2,1)S(1)} %collective-permute-done.3.fresh_ref.data_ref.own_ref.own_late, bf16[32,640]{1,0:T(8,128)(2,1)S(1)} %collective-permute-done.2.own_ref.other_first, ...), custom_call_target="tpu_custom_call" | custom-call | flops 1 | bytes 1 | tf_op jit(solution)/shard_map/pallas_call | solution.py:553
  15.1 0.2 %collective-permute-done.5.other_late = bf16[64,640]{1,0:T(8,128)(2,1)S(1)} collective-permute-done((bf16[64,640]{1,0:T(8,128)(2,1)S(1)}, bf16[64,640]{1,0:T(8,128)(2,1)S(1)}, u32[]{:S(2)}, u32[]{:S(2)}) %collective-permute-start.5) | collective-permute-done | bytes 81952 | tf_op jit(solution)/shard_map/ppermute | solution.py:514
  15.2 1.2 %shard_map.98 = f32[128,128]{1,0:T(8,128)} custom-call(f32[1]{0:T(128)S(6)} %copy.11.wave_ref, bf16[64,640]{1,0:T(8,128)(2,1)S(1)} %pad_maximum_fusion.own_ref.own_early, bf16[64,640]{1,0:T(8,128)(2,1)S(1)} %collective-permute-done.3.fresh_ref.data_ref.own_ref.own_late, bf16[32,640]{1,0:T(8,128)(2,1)S(1)} %collective-permute-done.2.own_ref.other_first, ...), custom_call_target="tpu_custom_call" | custom-call | tf_op jit(solution)/shard_map/pallas_call | solution.py:562
  (4 shorter events, 0.0 us)
Async XLA Ops:
  1.2 4.2 %copy-start = (f32[6,256]{1,0:T(8,128)S(1)}, f32[6,256]{1,0:T(8,128)}, u32[]{:S(2)}) copy-start(f32[6,256]{1,0:T(8,128)} %tgeom_ref.11) | copy-start | bytes 18436
  1.2 5.1 %collective-permute-start = (bf16[16,640]{1,0:T(8,128)(2,1)S(1)}, bf16[16,640]{1,0:T(8,128)(2,1)S(1)}, u32[]{:S(2)}, u32[]{:S(2)}) collective-permute-start(bf16[16,640]{1,0:T(8,128)(2,1)S(1)} %get-tuple-element.34.data_ref.own_ref), channel_id=1, source_target_pairs={{0,9},{1,8},{2,11},{3,10},{4,13},{5,12},{6,15},{7,14},{8,1},{9,0},... | collective-permute-start | bytes 61448 | tf_op jit(solution)/shard_map/ppermute | solution.py:514
  6.3 3.5 %collective-permute-start.1 = (bf16[32,640]{1,0:T(8,128)(2,1)S(1)}, bf16[32,640]{1,0:T(8,128)(2,1)S(1)}, u32[]{:S(2)}, u32[]{:S(2)}) collective-permute-start(bf16[32,640]{1,0:T(8,128)(2,1)S(1)} %constant_dynamic-update-slice_fusion.own_ref), channel_id=1, source_target_pairs={{0,5},{1,2},{2,1},{3,6},{4,7},{5,0},{6,3},{7,4},{8,11},{9,12},{10,... | collective-permute-start | bytes 122888 | tf_op jit(solution)/shard_map/ppermute | solution.py:514
  8.8 1.3 %collective-permute-start.2 = (bf16[32,640]{1,0:T(8,128)(2,1)S(1)}, bf16[32,640]{1,0:T(8,128)(2,1)S(1)}, u32[]{:S(2)}, u32[]{:S(2)}) collective-permute-start(bf16[32,640]{1,0:T(8,128)(2,1)S(1)} %get-tuple-element.39), channel_id=1, source_target_pairs={{0,1},{1,0},{2,3},{3,2},{4,5},{5,4},{6,7},{7,6},{8,9},{9,8},{10,11... | collective-permute-start | bytes 122888 | tf_op jit(solution)/shard_map/ppermute | solution.py:514
  10.1 3.9 %collective-permute-start.3 = (bf16[64,640]{1,0:T(8,128)(2,1)S(1)}, bf16[64,640]{1,0:T(8,128)(2,1)S(1)}, u32[]{:S(2)}, u32[]{:S(2)}) collective-permute-start(bf16[64,640]{1,0:T(8,128)(2,1)S(1)} %pad_maximum_fusion.own_ref.own_early), channel_id=1, source_target_pairs={{0,3},{1,4},{2,7},{3,0},{4,1},{5,6},{6,5},{7,2},{8,13},{9,10},{10,... | collective-permute-start | bytes 245768 | tf_op jit(solution)/shard_map/ppermute | solution.py:514
  11.6 1.3 %collective-permute-start.4 = (bf16[32,640]{1,0:T(8,128)(2,1)S(1)}, bf16[32,640]{1,0:T(8,128)(2,1)S(1)}, u32[]{:S(2)}, u32[]{:S(2)}) collective-permute-start(bf16[32,640]{1,0:T(8,128)(2,1)S(1)} %slice.3), channel_id=1, source_target_pairs={{0,1},{1,0},{2,3},{3,2},{4,5},{5,4},{6,7},{7,6},{8,9},{9,8},{10,11... | collective-permute-start | bytes 122888 | tf_op jit(solution)/shard_map/ppermute | solution.py:514
  13.9 1.3 %collective-permute-start.5 = (bf16[64,640]{1,0:T(8,128)(2,1)S(1)}, bf16[64,640]{1,0:T(8,128)(2,1)S(1)}, u32[]{:S(2)}, u32[]{:S(2)}) collective-permute-start(bf16[64,640]{1,0:T(8,128)(2,1)S(1)} %collective-permute-done.3.fresh_ref.data_ref.own_ref.own_late), channel_id=1, source_target_pairs={{0,1},{1,0},{2,3},{3,2},{4,5},{5,4},{6,7},{7,6},{8,9},{9,8},{10,11... | collective-permute-start | bytes 245768 | tf_op jit(solution)/shard_map/ppermute | solution.py:514

commit v3 on v1

--- a/solution.py
+++ b/solution.py
@@ -355,9 +355,32 @@
     near_kernel(exc, first, wave_ref, found_ref, data_ref, own_ref, target_ref, ut_ref, tgeom_ref, *refs)
 
 
+def weight_rows(data):
+    sign = jnp.where(iota((1, LANES), 1) < QSTEP, 1.0, -1.0).astype(BF16)
+    w = [data[:, i * LANES : (i + 1) * LANES] for i in range(3)]
+    swapped = jnp.concatenate([w[2][:, QSTEP:], w[2][:, :QSTEP]], 1)
+    return jnp.concatenate([w[0], -w[1], w[2] * sign], 1), jnp.concatenate([w[1], w[0], swapped], 1)
+
+
+def near_rows(left, v):
+    product = dot(left, v)
+    return (product[:, :LANES] + product[:, LANES:]) * INV_FOUR_PI
+
+
+def known_kernel(own_ref, other_ref, *refs):
+    *v_refs, out_ref = refs
+    cpd = 16
+    own_re, own_im = weight_rows(own_ref[: other_ref.shape[0]])
+    other_re, other_im = weight_rows(other_ref[...])
+    for k, v in enumerate([ref.at[i] for ref in v_refs for i in range(ref.shape[0])]):
+        here = slice(k * cpd, (k + 1) * cpd)
+        left = jnp.concatenate([own_re[here], other_re[here], own_im[here], other_im[here]], 0)
+        out_ref[k] = near_rows(left, v[...])
+
+
 def last_kernel(
     exc, partner, wave_ref, own_early, own_late, other_first, other_early, other_late, tgeom_ref,
-    early_re_ref, early_im_ref, *refs
+    known_early, known_late, early_re_ref, early_im_ref, *refs
 ):
     own = jnp.concatenate([own_early[...], own_late[...]], 0)
     other = jnp.concatenate([other_first[...], other_early[...], other_late[...]], 0)
@@ -369,13 +392,7 @@
     cpd = 16
     main = LANES
     slots = len(partner)
-    sign = jnp.where(lax.broadcasted_iota(jnp.int32, (1, LANES), 1) < QSTEP, 1.0, -1.0).astype(BF16)
-
-    def weight_rows(data):
-        w = [data[:, i * main : (i + 1) * main] for i in range(3)]
-        swapped = jnp.concatenate([w[2][:, QSTEP:], w[2][:, :QSTEP]], 1)
-        return jnp.concatenate([w[0], -w[1], w[2] * sign], 1), jnp.concatenate([w[1], w[0], swapped], 1)
-
+    quarter = slots // 4
     own_re, own_im = weight_rows(own)
     other_re, other_im = weight_rows(other)
     slot = 0
@@ -383,9 +400,11 @@
         for i in range(v_ref.shape[0]):
             here = slice(slot * cpd, (slot + 1) * cpd)
             there = slice(partner[slot] * cpd, (partner[slot] + 1) * cpd)
-            left = jnp.concatenate([own_re[here], other_re[there], own_im[here], other_im[there]], 0)
-            product = dot(left, v_ref[i])
-            a = (product[:, :LANES] + product[:, LANES:]) * INV_FOUR_PI
+            if slot // quarter in (0, 2):
+                a = (known_late if slot // quarter else known_early)[slot % quarter]
+            else:
+                left = jnp.concatenate([own_re[here], other_re[there], own_im[here], other_im[there]], 0)
+                a = near_rows(left, v_ref[i])
             there = slice((slots + partner[slot]) * cpd, (slots + partner[slot] + 1) * cpd)
             zre[here] = a[0:cpd]
             zre[there] = a[cpd : 2 * cpd]
@@ -504,7 +523,7 @@
         if not done:
             ut = made[4]
         if step == len(steps) - 2:
-            other_first = moved(made[3], 1, 1)
+            other_first = moved(own, 1, 1)
         done += slots
         fresh = arriving
         if not last:
@@ -517,24 +536,37 @@
     early = near_blocks(
         exc, done, quarter, wavenumber, found, other_early, other_early, target, ut, tgt_geom, False
     )
-    fresh, early, made = lax.optimization_barrier((fresh, early, made))
+
+    def known_rows(mine, others, *v):
+        return pl.pallas_call(
+            known_kernel,
+            out_shape=pltpu.VMEM((quarter, 4 * cpd, rows_here), F32),
+            in_specs=[VMEM_SPEC] * (2 + len(v)),
+            out_specs=VMEM_SPEC,
+            compiler_params=SMALL,
+            cost_estimate=pl.CostEstimate(flops=1, bytes_accessed=1, transcendentals=0),
+        )(*[in_vmem(x) for x in (mine, others, *v)])
+
+    known_early = known_rows(own, other_first, *near[: 3 * (len(steps) - 1) : 3])
+    fresh, early, made, known_early = lax.optimization_barrier((fresh, early, made, known_early))
     other_late = moved(fresh, 1, 1)
     late = near_blocks(
         exc, done + quarter, quarter, wavenumber, found, fresh, fresh, target, ut, tgt_geom, False
     )
     near.append(early[0])
     near.extend(late)
+    known_late = known_rows(fresh, other_early, early[0])
     partner = [units[1].index(u) for u in units[0]]
     return pl.pallas_call(
         functools.partial(last_kernel, exc, partner),
         out_shape=jax.ShapeDtypeStruct((rows_here, exc), F32),
-        in_specs=[SMEM_SPEC] + [VMEM_SPEC] * (8 + len(near)),
+        in_specs=[SMEM_SPEC] + [VMEM_SPEC] * (10 + len(near)),
         out_specs=VMEM_SPEC,
         scratch_shapes=[pltpu.VMEM((count * cpd, rows_here), F32)] * 2,
         compiler_params=SMALL,
     )(
         wavenumber,
-        *[in_vmem(x) for x in (own, fresh, other_first, other_early, other_late, tgt_geom, *early[1:], *near)],
+        *[in_vmem(x) for x in (own, fresh, other_first, other_early, other_late, tgt_geom, known_early, known_late, *early[1:], *near)],
     )
 
 

time: 16.8 us -> 16.6 us (0.988)
  waiting for transfers between devices: 2.6 us -> 2.22 us
    pallas_call x0 -> x2, Pallas kernels: none -> 0.39 us  [known_rows(): pl.pallas_call(known_kernel, out_shape=pltpu.VMEM((quarter, 4 * cpd, rows...]
    ppermute x6, waiting for transfers between devices: 2.6 us -> 2.22 us  [moved(): return lax.ppermute(value, ('row', 'col'), pairs)]
  transfers between devices with their start and end apart: 6 -> 6, of which waited for: 6 -> 4; matrix products, arithmetic and copies ran while one was open for 0% -> 0% of each run, Pallas kernels for 14% -> 16%
where the time goes in v3:
time: 16.6 us; the launch traced here: 16.4 us
  starting transfers between devices  8.42 us (51%)
  Pallas kernels  4.98 us (30%)
  waiting for transfers between devices  2.22 us (13%)
  between operations  0.76 us (5%)
    ppermute x6, starting transfers between devices, moved(): return lax.ppermute(value, ('row', 'col'), pairs)  8.42 us
    ppermute x6, waiting for transfers between devices, moved(): return lax.ppermute(value, ('row', 'col'), pairs)  2.22 us
    pallas_call x5, Pallas kernels, near_blocks(): pl.pallas_call(functools.partial(near_kernel if first else first_near_ker...  2.19 us
    pallas_call x1, Pallas kernels, exchanged(): pl.pallas_call(functools.partial(last_kernel, exc, partner), out_shape=ja...  1.23 us
    pallas_call x1, Pallas kernels, packed(): pl.pallas_call(functools.partial(pack_kernel, units), out_shape=[pltpu.VM...  1.17 us
    pallas_call x2, Pallas kernels, known_rows(): pl.pallas_call(known_kernel, out_shape=pltpu.VMEM((quarter, 4 * cpd, rows...  0.39 us
  transfers between devices with their start and end apart: 6, of which 4 were waited for; matrix products, arithmetic and copies ran while one was open for 0% of the time, Pallas kernels for 16%

profile of v3, /device:TPU:0, one launch (start us, length us, event | category | flops | bytes accessed | tf_op | source)
XLA Modules:
  0.0 16.4 jit_solution(9582253556529254022)
XLA Ops:
  0.0 1.2 %shard_map.91 = (bf16[16,640]{1,0:T(8,128)(2,1)S(1)}, f32[3,8,128]{2,1,0:T(8,128)S(1)}, bf16[2,192,128]{2,1,0:T(8,128)(2,1)S(1)}, s32[8]{0:T(128)S(4)}) custom-call(s32[2,9]{1,0:T(2,128)} %order_hbm.1, f32[4,16]{1,0:T(4,128)} %geom_hbm.1, bf16[16,128]{1,0:T(8,128)(2,1)} %bitcast.3, f32[3,192]{1,0:T(4,128)} %nodes_hbm.1, bf16[2,16,192]{2,1,0:T(8,128)(2,1)} %bitcast.2, ...), custom_call_target="tpu_custom_call" | custom-call | tf_op jit(solution)/shard_map/pallas_call | solution.py:458
  1.2 0.0 copy-start
  1.2 3.5 %collective-permute-start = (bf16[16,640]{1,0:T(8,128)(2,1)S(1)}, bf16[16,640]{1,0:T(8,128)(2,1)S(1)}, u32[]{:S(2)}, u32[]{:S(2)}) collective-permute-start(bf16[16,640]{1,0:T(8,128)(2,1)S(1)} %get-tuple-element.35.data_ref.own_ref), channel_id=1, source_target_pairs={{0,9},{1,8},{2,11},{3,10},{4,13},{5,12},{6,15},{7,14},{8,1},{9,0},... | collective-permute-start | bytes 61448 | tf_op jit(solution)/shard_map/ppermute | solution.py:508
  5.4 0.0 copy-done
  5.4 0.4 %shard_map.92 = (bf16[1,384,256]{2,1,0:T(8,128)(2,1)S(1)}, bf16[16,128]{1,0:T(8,128)(2,1)S(1)}, bf16[16,128]{1,0:T(8,128)(2,1)S(1)}, bf16[16,640]{1,0:T(8,128)(2,1)S(1)}, bf16[384,256]{1,0:T(8,128)(2,1)S(1)}) custom-call(f32[1]{0:T(128)S(6)} %copy.11.wave_ref, s32[8]{0:T(128)S(4)} %get-tuple-element.34.found_ref, ...), custom_call_target="tpu_custom_call" | custom-call | flops 1 | bytes 1 | tf_op jit(solution)/shard_map/pallas_call | solution.py:482
  5.9 0.4 %collective-permute-done.data_ref = bf16[16,640]{1,0:T(8,128)(2,1)S(1)} collective-permute-done((bf16[16,640]{1,0:T(8,128)(2,1)S(1)}, bf16[16,640]{1,0:T(8,128)(2,1)S(1)}, u32[]{:S(2)}, u32[]{:S(2)}) %collective-permute-start) | collective-permute-done | bytes 20512 | tf_op jit(solution)/shard_map/ppermute | solution.py:508
  6.3 1.9 %collective-permute-start.1 = (bf16[32,640]{1,0:T(8,128)(2,1)S(1)}, bf16[32,640]{1,0:T(8,128)(2,1)S(1)}, u32[]{:S(2)}, u32[]{:S(2)}) collective-permute-start(bf16[32,640]{1,0:T(8,128)(2,1)S(1)} %constant_dynamic-update-slice_fusion.own_ref), channel_id=1, source_target_pairs={{0,5},{1,2},{2,1},{3,6},{4,7},{5,0},{6,3},{7,4},{8,11},{9,12},{10,... | collective-permute-start | bytes 122888 | tf_op jit(solution)/shard_map/ppermute | solution.py:508
  8.1 0.3 %collective-permute-start.2 = (bf16[32,640]{1,0:T(8,128)(2,1)S(1)}, bf16[32,640]{1,0:T(8,128)(2,1)S(1)}, u32[]{:S(2)}, u32[]{:S(2)}) collective-permute-start(bf16[32,640]{1,0:T(8,128)(2,1)S(1)} %constant_dynamic-update-slice_fusion.own_ref), channel_id=1, source_target_pairs={{0,1},{1,0},{2,3},{3,2},{4,5},{5,4},{6,7},{7,6},{8,9},{9,8},{10,11... | collective-permute-start | bytes 122888 | tf_op jit(solution)/shard_map/ppermute | solution.py:508
  8.4 0.2 %shard_map.93 = (bf16[1,384,256]{2,1,0:T(8,128)(2,1)S(1)}, bf16[16,128]{1,0:T(8,128)(2,1)S(1)}, bf16[16,128]{1,0:T(8,128)(2,1)S(1)}, bf16[32,640]{1,0:T(8,128)(2,1)S(1)}) custom-call(f32[1]{0:T(128)S(6)} %copy.11.wave_ref, s32[8]{0:T(128)S(4)} %get-tuple-element.34.found_ref, bf16[16,640]{1,0:T(8,128)(2,1)S(1)} %collective-permute-done.data_ref, ...), custom_call_target="tpu_custom_call" | custom-call | flops 1 | bytes 1 | tf_op jit(solution)/shard_map/pallas_call | solution.py:482
  8.6 1.2 %collective-permute-done.1.data_ref = bf16[32,640]{1,0:T(8,128)(2,1)S(1)} collective-permute-done((bf16[32,640]{1,0:T(8,128)(2,1)S(1)}, bf16[32,640]{1,0:T(8,128)(2,1)S(1)}, u32[]{:S(2)}, u32[]{:S(2)}) %collective-permute-start.1) | collective-permute-done | bytes 40992 | tf_op jit(solution)/shard_map/ppermute | solution.py:508
  9.8 0.0 collective-permute-done.2.own_ref.other_ref.other_first
  9.8 1.7 %collective-permute-start.3 = (bf16[64,640]{1,0:T(8,128)(2,1)S(1)}, bf16[64,640]{1,0:T(8,128)(2,1)S(1)}, u32[]{:S(2)}, u32[]{:S(2)}) collective-permute-start(bf16[64,640]{1,0:T(8,128)(2,1)S(1)} %pad_maximum_fusion.own_ref.own_early), channel_id=1, source_target_pairs={{0,3},{1,4},{2,7},{3,0},{4,1},{5,6},{6,5},{7,2},{8,13},{9,10},{10,... | collective-permute-start | bytes 245768 | tf_op jit(solution)/shard_map/ppermute | solution.py:508
  11.6 0.5 %collective-permute-start.4 = (bf16[32,640]{1,0:T(8,128)(2,1)S(1)}, bf16[32,640]{1,0:T(8,128)(2,1)S(1)}, u32[]{:S(2)}, u32[]{:S(2)}) collective-permute-start(bf16[32,640]{1,0:T(8,128)(2,1)S(1)} %slice.3), channel_id=1, source_target_pairs={{0,1},{1,0},{2,3},{3,2},{4,5},{5,4},{6,7},{7,6},{8,9},{9,8},{10,11... | collective-permute-start | bytes 122888 | tf_op jit(solution)/shard_map/ppermute | solution.py:508
  12.0 0.2 %shard_map.96.known_early = f32[2,64,128]{2,1,0:T(8,128)S(1)} custom-call(bf16[64,640]{1,0:T(8,128)(2,1)S(1)} %pad_maximum_fusion.own_ref.own_early, bf16[32,640]{1,0:T(8,128)(2,1)S(1)} %collective-permute-done.2.own_ref.other_ref.other_first, bf16[1,384,256]{2,1,0:T(8,128)(2,1)S(1)} %get-tuple-element.49.refs_0_, ...), custom_call_target="tpu_custom_call" | custom-call | flops 1 | bytes 1 | tf_op jit(solution)/shard_map/pallas_call | solution.py:541
  12.2 0.8 %shard_map.95 = (bf16[2,384,256]{2,1,0:T(8,128)(2,1)S(1)}, bf16[64,128]{1,0:T(8,128)(2,1)S(1)}, bf16[64,128]{1,0:T(8,128)(2,1)S(1)}) custom-call(f32[1]{0:T(128)S(6)} %copy.11.wave_ref, s32[8]{0:T(128)S(4)} %get-tuple-element.34.found_ref, bf16[32,640]{1,0:T(8,128)(2,1)S(1)} %collective-permute-done.1.data_ref, ...), custom_call_target="tpu_custom_call" | custom-call | flops 1 | bytes 1 | tf_op jit(solution)/shard_map/pallas_call | solution.py:482
  13.0 0.0 collective-permute-done.4.data_ref.own_ref.other_ref.other_early
  13.0 0.5 %shard_map.94 = (bf16[2,384,256]{2,1,0:T(8,128)(2,1)S(1)}, bf16[32,128]{1,0:T(8,128)(2,1)S(1)}, bf16[32,128]{1,0:T(8,128)(2,1)S(1)}) custom-call(f32[1]{0:T(128)S(6)} %copy.11.wave_ref, s32[8]{0:T(128)S(4)} %get-tuple-element.34.found_ref, bf16[32,640]{1,0:T(8,128)(2,1)S(1)} %collective-permute-done.4.data_ref.own_ref.other_ref.other_early, ...), custom_call_target="tpu_custom_call" | custom-call | flops 1 | bytes 1 | tf_op jit(solution)/shard_map/pallas_call | solution.py:482
  13.5 0.2 %collective-permute-done.3.own_ref.data_ref.own_late = bf16[64,640]{1,0:T(8,128)(2,1)S(1)} collective-permute-done((bf16[64,640]{1,0:T(8,128)(2,1)S(1)}, bf16[64,640]{1,0:T(8,128)(2,1)S(1)}, u32[]{:S(2)}, u32[]{:S(2)}) %collective-permute-start.3) | collective-permute-done | bytes 81952 | tf_op jit(solution)/shard_map/ppermute | solution.py:508
  13.8 0.5 %collective-permute-start.5 = (bf16[64,640]{1,0:T(8,128)(2,1)S(1)}, bf16[64,640]{1,0:T(8,128)(2,1)S(1)}, u32[]{:S(2)}, u32[]{:S(2)}) collective-permute-start(bf16[64,640]{1,0:T(8,128)(2,1)S(1)} %collective-permute-done.3.own_ref.data_ref.own_late), channel_id=1, source_target_pairs={{0,1},{1,0},{2,3},{3,2},{4,5},{5,4},{6,7},{7,6},{8,9},{9,8},{10,11... | collective-permute-start | bytes 245768 | tf_op jit(solution)/shard_map/ppermute | solution.py:508
  14.3 0.3 %shard_map.98 = (bf16[2,384,256]{2,1,0:T(8,128)(2,1)S(1)}, bf16[64,128]{1,0:T(8,128)(2,1)S(1)}, bf16[64,128]{1,0:T(8,128)(2,1)S(1)}) custom-call(f32[1]{0:T(128)S(6)} %copy.11.wave_ref, s32[8]{0:T(128)S(4)} %get-tuple-element.34.found_ref, bf16[64,640]{1,0:T(8,128)(2,1)S(1)} %collective-permute-done.3.own_ref.data_ref.own_late, ...), custom_call_target="tpu_custom_call" | custom-call | flops 1 | bytes 1 | tf_op jit(solution)/shard_map/pallas_call | solution.py:482
  14.5 0.2 %shard_map.97.known_late = f32[2,64,128]{2,1,0:T(8,128)S(1)} custom-call(bf16[64,640]{1,0:T(8,128)(2,1)S(1)} %collective-permute-done.3.own_ref.data_ref.own_late, bf16[32,640]{1,0:T(8,128)(2,1)S(1)} %collective-permute-done.4.data_ref.own_ref.other_ref.other_early, bf16[2,384,256]{2,1,0:T(8,128)(2,1)S(1)} %get-tuple-element.53.refs_0_.refs_9_), custom_call_target="tpu_custom_call" | custom-call | flops 1 | bytes 1 | tf_op jit(solution)/shard_map/pallas_call | solution.py:541
  14.8 0.4 %collective-permute-done.5.other_late = bf16[64,640]{1,0:T(8,128)(2,1)S(1)} collective-permute-done((bf16[64,640]{1,0:T(8,128)(2,1)S(1)}, bf16[64,640]{1,0:T(8,128)(2,1)S(1)}, u32[]{:S(2)}, u32[]{:S(2)}) %collective-permute-start.5) | collective-permute-done | bytes 81952 | tf_op jit(solution)/shard_map/ppermute | solution.py:508
  15.2 1.2 %shard_map.99 = f32[128,128]{1,0:T(8,128)} custom-call(f32[1]{0:T(128)S(6)} %copy.11.wave_ref, bf16[64,640]{1,0:T(8,128)(2,1)S(1)} %pad_maximum_fusion.own_ref.own_early, bf16[64,640]{1,0:T(8,128)(2,1)S(1)} %collective-permute-done.3.own_ref.data_ref.own_late, bf16[32,640]{1,0:T(8,128)(2,1)S(1)} %collective-permute-done.2.own_ref.other_ref.other_first, ...), custom_call_target="tpu_custom_call" | custom-call | tf_op jit(solution)/shard_map/pallas_call | solution.py:560
  (4 shorter events, 0.0 us)
Async XLA Ops:
  1.2 4.2 %copy-start = (f32[6,256]{1,0:T(8,128)S(1)}, f32[6,256]{1,0:T(8,128)}, u32[]{:S(2)}) copy-start(f32[6,256]{1,0:T(8,128)} %tgeom_ref.11) | copy-start | bytes 18436
  1.2 5.1 %collective-permute-start = (bf16[16,640]{1,0:T(8,128)(2,1)S(1)}, bf16[16,640]{1,0:T(8,128)(2,1)S(1)}, u32[]{:S(2)}, u32[]{:S(2)}) collective-permute-start(bf16[16,640]{1,0:T(8,128)(2,1)S(1)} %get-tuple-element.35.data_ref.own_ref), channel_id=1, source_target_pairs={{0,9},{1,8},{2,11},{3,10},{4,13},{5,12},{6,15},{7,14},{8,1},{9,0},... | collective-permute-start | bytes 61448 | tf_op jit(solution)/shard_map/ppermute | solution.py:508
  6.3 3.5 %collective-permute-start.1 = (bf16[32,640]{1,0:T(8,128)(2,1)S(1)}, bf16[32,640]{1,0:T(8,128)(2,1)S(1)}, u32[]{:S(2)}, u32[]{:S(2)}) collective-permute-start(bf16[32,640]{1,0:T(8,128)(2,1)S(1)} %constant_dynamic-update-slice_fusion.own_ref), channel_id=1, source_target_pairs={{0,5},{1,2},{2,1},{3,6},{4,7},{5,0},{6,3},{7,4},{8,11},{9,12},{10,... | collective-permute-start | bytes 122888 | tf_op jit(solution)/shard_map/ppermute | solution.py:508
  8.1 1.7 %collective-permute-start.2 = (bf16[32,640]{1,0:T(8,128)(2,1)S(1)}, bf16[32,640]{1,0:T(8,128)(2,1)S(1)}, u32[]{:S(2)}, u32[]{:S(2)}) collective-permute-start(bf16[32,640]{1,0:T(8,128)(2,1)S(1)} %constant_dynamic-update-slice_fusion.own_ref), channel_id=1, source_target_pairs={{0,1},{1,0},{2,3},{3,2},{4,5},{5,4},{6,7},{7,6},{8,9},{9,8},{10,11... | collective-permute-start | bytes 122888 | tf_op jit(solution)/shard_map/ppermute | solution.py:508
  9.8 3.9 %collective-permute-start.3 = (bf16[64,640]{1,0:T(8,128)(2,1)S(1)}, bf16[64,640]{1,0:T(8,128)(2,1)S(1)}, u32[]{:S(2)}, u32[]{:S(2)}) collective-permute-start(bf16[64,640]{1,0:T(8,128)(2,1)S(1)} %pad_maximum_fusion.own_ref.own_early), channel_id=1, source_target_pairs={{0,3},{1,4},{2,7},{3,0},{4,1},{5,6},{6,5},{7,2},{8,13},{9,10},{10,... | collective-permute-start | bytes 245768 | tf_op jit(solution)/shard_map/ppermute | solution.py:508
  11.6 1.4 %collective-permute-start.4 = (bf16[32,640]{1,0:T(8,128)(2,1)S(1)}, bf16[32,640]{1,0:T(8,128)(2,1)S(1)}, u32[]{:S(2)}, u32[]{:S(2)}) collective-permute-start(bf16[32,640]{1,0:T(8,128)(2,1)S(1)} %slice.3), channel_id=1, source_target_pairs={{0,1},{1,0},{2,3},{3,2},{4,5},{5,4},{6,7},{7,6},{8,9},{9,8},{10,11... | collective-permute-start | bytes 122888 | tf_op jit(solution)/shard_map/ppermute | solution.py:508
  13.8 1.4 %collective-permute-start.5 = (bf16[64,640]{1,0:T(8,128)(2,1)S(1)}, bf16[64,640]{1,0:T(8,128)(2,1)S(1)}, u32[]{:S(2)}, u32[]{:S(2)}) collective-permute-start(bf16[64,640]{1,0:T(8,128)(2,1)S(1)} %collective-permute-done.3.own_ref.data_ref.own_late), channel_id=1, source_target_pairs={{0,1},{1,0},{2,3},{3,2},{4,5},{5,4},{6,7},{7,6},{8,9},{9,8},{10,11... | collective-permute-start | bytes 245768 | tf_op jit(solution)/shard_map/ppermute | solution.py:508

commit v4 on v3

--- a/solution.py
+++ b/solution.py
@@ -311,14 +311,11 @@
 
 
 def far_rows(data, exc, wave, tgeom):
-    shape = (LANES, 4 * LANES)
-    at, wanted = iota(shape, 0) - geom_lane(16), lax.div(iota(shape, 1), LANES)
-    pick = jnp.logical_and(
-        jnp.logical_and(at >= 0, at < 4 * PARTS), lax.rem(at + 4 * LANES, 4) == wanted
-    )
-    geom = data[:, EXC_AT + exc :]
-    spread = dot(geom, jnp.where(pick, 1.0, 0.0).astype(BF16))
-    return far_kernel_values(wave, [spread[:, i * LANES : (i + 1) * LANES] for i in range(4)], tgeom)
+    at = geom_lane(16)
+    geom = data[:, EXC_AT + exc :].astype(F32)
+    parts = [geom[:, at + 4 * i : at + 4 * i + 4] for i in range(PARTS)]
+    total = (parts[0] + parts[1]) + parts[2]
+    return far_kernel_values(wave, [total[:, i : i + 1] for i in range(4)], tgeom)
 
 
 def own_targets(tgeom_ref, rows):

time: 16.6 us -> 16.6 us (level)
  Pallas kernels: 4.98 us -> 5.53 us
  waiting for transfers between devices: 2.22 us -> 1.71 us
    pallas_call x5, Pallas kernels: 2.19 us -> 2.76 us  [near_blocks(): pl.pallas_call(functools.partial(near_kernel if first else first_near_ker...]
    ppermute x6, waiting for transfers between devices: 2.22 us -> 1.71 us  [moved(): return lax.ppermute(value, ('row', 'col'), pairs)]
  transfers between devices with their start and end apart: 6 -> 6, of which waited for: 4 -> 4; matrix products, arithmetic and copies ran while one was open for 0% -> 0% of each run, Pallas kernels for 16% -> 19%
where the time goes in v4:
time: 16.6 us; the launch traced here: 16.5 us
  starting transfers between devices  8.42 us (51%)
  Pallas kernels  5.53 us (33%)
  waiting for transfers between devices  1.71 us (10%)
  between operations  0.76 us (5%)
    ppermute x6, starting transfers between devices, moved(): return lax.ppermute(value, ('row', 'col'), pairs)  8.42 us
    pallas_call x5, Pallas kernels, near_blocks(): pl.pallas_call(functools.partial(near_kernel if first else first_near_ker...  2.76 us
    ppermute x6, waiting for transfers between devices, moved(): return lax.ppermute(value, ('row', 'col'), pairs)  1.71 us
    pallas_call x1, Pallas kernels, exchanged(): pl.pallas_call(functools.partial(last_kernel, exc, partner), out_shape=ja...  1.2 us
    pallas_call x1, Pallas kernels, packed(): pl.pallas_call(functools.partial(pack_kernel, units), out_shape=[pltpu.VM...  1.17 us
    pallas_call x2, Pallas kernels, known_rows(): pl.pallas_call(known_kernel, out_shape=pltpu.VMEM((quarter, 4 * cpd, rows...  0.39 us
  transfers between devices with their start and end apart: 6, of which 4 were waited for; matrix products, arithmetic and copies ran while one was open for 0% of the time, Pallas kernels for 19%

profile of v4, /device:TPU:0, one launch (start us, length us, event | category | flops | bytes accessed | tf_op | source)
XLA Modules:
  0.0 16.5 jit_solution(2296981986978381439)
XLA Ops:
  0.0 1.2 %shard_map.91 = (bf16[16,640]{1,0:T(8,128)(2,1)S(1)}, f32[3,8,128]{2,1,0:T(8,128)S(1)}, bf16[2,192,128]{2,1,0:T(8,128)(2,1)S(1)}, s32[8]{0:T(128)S(4)}) custom-call(s32[2,9]{1,0:T(2,128)} %order_hbm.1, f32[4,16]{1,0:T(4,128)} %geom_hbm.1, bf16[16,128]{1,0:T(8,128)(2,1)} %bitcast.3, f32[3,192]{1,0:T(4,128)} %nodes_hbm.1, bf16[2,16,192]{2,1,0:T(8,128)(2,1)} %bitcast.2, ...), custom_call_target="tpu_custom_call" | custom-call | tf_op jit(solution)/shard_map/pallas_call | solution.py:455
  1.2 0.0 copy-start
  1.2 3.5 %collective-permute-start = (bf16[16,640]{1,0:T(8,128)(2,1)S(1)}, bf16[16,640]{1,0:T(8,128)(2,1)S(1)}, u32[]{:S(2)}, u32[]{:S(2)}) collective-permute-start(bf16[16,640]{1,0:T(8,128)(2,1)S(1)} %get-tuple-element.35.data_ref.own_ref), channel_id=1, source_target_pairs={{0,9},{1,8},{2,11},{3,10},{4,13},{5,12},{6,15},{7,14},{8,1},{9,0},... | collective-permute-start | bytes 61448 | tf_op jit(solution)/shard_map/ppermute | solution.py:505
  5.4 0.0 copy-done
  5.4 0.7 %shard_map.92 = (bf16[1,384,256]{2,1,0:T(8,128)(2,1)S(1)}, bf16[16,128]{1,0:T(8,128)(2,1)S(1)}, bf16[16,128]{1,0:T(8,128)(2,1)S(1)}, bf16[16,640]{1,0:T(8,128)(2,1)S(1)}, bf16[384,256]{1,0:T(8,128)(2,1)S(1)}) custom-call(f32[1]{0:T(128)S(6)} %copy.11.wave_ref, s32[8]{0:T(128)S(4)} %get-tuple-element.34.found_ref, ...), custom_call_target="tpu_custom_call" | custom-call | flops 1 | bytes 1 | tf_op jit(solution)/shard_map/pallas_call | solution.py:479
  6.1 0.1 collective-permute-done.data_ref
  6.3 1.9 %collective-permute-start.1 = (bf16[32,640]{1,0:T(8,128)(2,1)S(1)}, bf16[32,640]{1,0:T(8,128)(2,1)S(1)}, u32[]{:S(2)}, u32[]{:S(2)}) collective-permute-start(bf16[32,640]{1,0:T(8,128)(2,1)S(1)} %constant_dynamic-update-slice_fusion.own_ref), channel_id=1, source_target_pairs={{0,5},{1,2},{2,1},{3,6},{4,7},{5,0},{6,3},{7,4},{8,11},{9,12},{10,... | collective-permute-start | bytes 122888 | tf_op jit(solution)/shard_map/ppermute | solution.py:505
  8.1 0.3 %collective-permute-start.2 = (bf16[32,640]{1,0:T(8,128)(2,1)S(1)}, bf16[32,640]{1,0:T(8,128)(2,1)S(1)}, u32[]{:S(2)}, u32[]{:S(2)}) collective-permute-start(bf16[32,640]{1,0:T(8,128)(2,1)S(1)} %constant_dynamic-update-slice_fusion.own_ref), channel_id=1, source_target_pairs={{0,1},{1,0},{2,3},{3,2},{4,5},{5,4},{6,7},{7,6},{8,9},{9,8},{10,11... | collective-permute-start | bytes 122888 | tf_op jit(solution)/shard_map/ppermute | solution.py:505
  8.4 0.5 %shard_map.93 = (bf16[1,384,256]{2,1,0:T(8,128)(2,1)S(1)}, bf16[16,128]{1,0:T(8,128)(2,1)S(1)}, bf16[16,128]{1,0:T(8,128)(2,1)S(1)}, bf16[32,640]{1,0:T(8,128)(2,1)S(1)}) custom-call(f32[1]{0:T(128)S(6)} %copy.11.wave_ref, s32[8]{0:T(128)S(4)} %get-tuple-element.34.found_ref, bf16[16,640]{1,0:T(8,128)(2,1)S(1)} %collective-permute-done.data_ref, ...), custom_call_target="tpu_custom_call" | custom-call | flops 1 | bytes 1 | tf_op jit(solution)/shard_map/pallas_call | solution.py:479
  8.9 0.9 %collective-permute-done.1.data_ref = bf16[32,640]{1,0:T(8,128)(2,1)S(1)} collective-permute-done((bf16[32,640]{1,0:T(8,128)(2,1)S(1)}, bf16[32,640]{1,0:T(8,128)(2,1)S(1)}, u32[]{:S(2)}, u32[]{:S(2)}) %collective-permute-start.1) | collective-permute-done | bytes 40992 | tf_op jit(solution)/shard_map/ppermute | solution.py:505
  9.8 0.0 collective-permute-done.2.own_ref.other_ref.other_first
  9.8 1.7 %collective-permute-start.3 = (bf16[64,640]{1,0:T(8,128)(2,1)S(1)}, bf16[64,640]{1,0:T(8,128)(2,1)S(1)}, u32[]{:S(2)}, u32[]{:S(2)}) collective-permute-start(bf16[64,640]{1,0:T(8,128)(2,1)S(1)} %pad_maximum_fusion.own_ref.own_early), channel_id=1, source_target_pairs={{0,3},{1,4},{2,7},{3,0},{4,1},{5,6},{6,5},{7,2},{8,13},{9,10},{10,... | collective-permute-start | bytes 245768 | tf_op jit(solution)/shard_map/ppermute | solution.py:505
  11.6 0.5 %collective-permute-start.4 = (bf16[32,640]{1,0:T(8,128)(2,1)S(1)}, bf16[32,640]{1,0:T(8,128)(2,1)S(1)}, u32[]{:S(2)}, u32[]{:S(2)}) collective-permute-start(bf16[32,640]{1,0:T(8,128)(2,1)S(1)} %slice.3), channel_id=1, source_target_pairs={{0,1},{1,0},{2,3},{3,2},{4,5},{5,4},{6,7},{7,6},{8,9},{9,8},{10,11... | collective-permute-start | bytes 122888 | tf_op jit(solution)/shard_map/ppermute | solution.py:505
  12.0 0.2 %shard_map.96.known_early = f32[2,64,128]{2,1,0:T(8,128)S(1)} custom-call(bf16[64,640]{1,0:T(8,128)(2,1)S(1)} %pad_maximum_fusion.own_ref.own_early, bf16[32,640]{1,0:T(8,128)(2,1)S(1)} %collective-permute-done.2.own_ref.other_ref.other_first, bf16[1,384,256]{2,1,0:T(8,128)(2,1)S(1)} %get-tuple-element.49.refs_0_, ...), custom_call_target="tpu_custom_call" | custom-call | flops 1 | bytes 1 | tf_op jit(solution)/shard_map/pallas_call | solution.py:538
  12.2 0.3 %shard_map.95 = (bf16[2,384,256]{2,1,0:T(8,128)(2,1)S(1)}, bf16[64,128]{1,0:T(8,128)(2,1)S(1)}, bf16[64,128]{1,0:T(8,128)(2,1)S(1)}) custom-call(f32[1]{0:T(128)S(6)} %copy.11.wave_ref, s32[8]{0:T(128)S(4)} %get-tuple-element.34.found_ref, bf16[32,640]{1,0:T(8,128)(2,1)S(1)} %collective-permute-done.1.data_ref, ...), custom_call_target="tpu_custom_call" | custom-call | flops 1 | bytes 1 | tf_op jit(solution)/shard_map/pallas_call | solution.py:479
  12.5 0.4 %collective-permute-done.4.data_ref.own_ref.other_ref.other_early = bf16[32,640]{1,0:T(8,128)(2,1)S(1)} collective-permute-done((bf16[32,640]{1,0:T(8,128)(2,1)S(1)}, bf16[32,640]{1,0:T(8,128)(2,1)S(1)}, u32[]{:S(2)}, u32[]{:S(2)}) %collective-permute-start.4) | collective-permute-done | bytes 40992 | tf_op jit(solution)/shard_map/ppermute | solution.py:505
  12.9 0.5 %shard_map.94 = (bf16[2,384,256]{2,1,0:T(8,128)(2,1)S(1)}, bf16[32,128]{1,0:T(8,128)(2,1)S(1)}, bf16[32,128]{1,0:T(8,128)(2,1)S(1)}) custom-call(f32[1]{0:T(128)S(6)} %copy.11.wave_ref, s32[8]{0:T(128)S(4)} %get-tuple-element.34.found_ref, bf16[32,640]{1,0:T(8,128)(2,1)S(1)} %collective-permute-done.4.data_ref.own_ref.other_ref.other_early, ...), custom_call_target="tpu_custom_call" | custom-call | flops 1 | bytes 1 | tf_op jit(solution)/shard_map/pallas_call | solution.py:479
  13.4 0.3 %collective-permute-done.3.own_ref.data_ref.own_late = bf16[64,640]{1,0:T(8,128)(2,1)S(1)} collective-permute-done((bf16[64,640]{1,0:T(8,128)(2,1)S(1)}, bf16[64,640]{1,0:T(8,128)(2,1)S(1)}, u32[]{:S(2)}, u32[]{:S(2)}) %collective-permute-start.3) | collective-permute-done | bytes 81952 | tf_op jit(solution)/shard_map/ppermute | solution.py:505
  13.8 0.5 %collective-permute-start.5 = (bf16[64,640]{1,0:T(8,128)(2,1)S(1)}, bf16[64,640]{1,0:T(8,128)(2,1)S(1)}, u32[]{:S(2)}, u32[]{:S(2)}) collective-permute-start(bf16[64,640]{1,0:T(8,128)(2,1)S(1)} %collective-permute-done.3.own_ref.data_ref.own_late), channel_id=1, source_target_pairs={{0,1},{1,0},{2,3},{3,2},{4,5},{5,4},{6,7},{7,6},{8,9},{9,8},{10,11... | collective-permute-start | bytes 245768 | tf_op jit(solution)/shard_map/ppermute | solution.py:505
  14.3 0.8 %shard_map.98 = (bf16[2,384,256]{2,1,0:T(8,128)(2,1)S(1)}, bf16[64,128]{1,0:T(8,128)(2,1)S(1)}, bf16[64,128]{1,0:T(8,128)(2,1)S(1)}) custom-call(f32[1]{0:T(128)S(6)} %copy.11.wave_ref, s32[8]{0:T(128)S(4)} %get-tuple-element.34.found_ref, bf16[64,640]{1,0:T(8,128)(2,1)S(1)} %collective-permute-done.3.own_ref.data_ref.own_late, ...), custom_call_target="tpu_custom_call" | custom-call | flops 1 | bytes 1 | tf_op jit(solution)/shard_map/pallas_call | solution.py:479
  15.0 0.2 %shard_map.97.known_late = f32[2,64,128]{2,1,0:T(8,128)S(1)} custom-call(bf16[64,640]{1,0:T(8,128)(2,1)S(1)} %collective-permute-done.3.own_ref.data_ref.own_late, bf16[32,640]{1,0:T(8,128)(2,1)S(1)} %collective-permute-done.4.data_ref.own_ref.other_ref.other_early, bf16[2,384,256]{2,1,0:T(8,128)(2,1)S(1)} %get-tuple-element.53.refs_0_.refs_9_), custom_call_target="tpu_custom_call" | custom-call | flops 1 | bytes 1 | tf_op jit(solution)/shard_map/pallas_call | solution.py:538
  15.2 0.0 collective-permute-done.5.other_late
  15.3 1.2 %shard_map.99 = f32[128,128]{1,0:T(8,128)} custom-call(f32[1]{0:T(128)S(6)} %copy.11.wave_ref, bf16[64,640]{1,0:T(8,128)(2,1)S(1)} %pad_maximum_fusion.own_ref.own_early, bf16[64,640]{1,0:T(8,128)(2,1)S(1)} %collective-permute-done.3.own_ref.data_ref.own_late, bf16[32,640]{1,0:T(8,128)(2,1)S(1)} %collective-permute-done.2.own_ref.other_ref.other_first, ...), custom_call_target="tpu_custom_call" | custom-call | tf_op jit(solution)/shard_map/pallas_call | solution.py:557
  (4 shorter events, 0.0 us)
Async XLA Ops:
  1.2 4.2 %copy-start = (f32[6,256]{1,0:T(8,128)S(1)}, f32[6,256]{1,0:T(8,128)}, u32[]{:S(2)}) copy-start(f32[6,256]{1,0:T(8,128)} %tgeom_ref.11) | copy-start | bytes 18436
  1.2 5.1 %collective-permute-start = (bf16[16,640]{1,0:T(8,128)(2,1)S(1)}, bf16[16,640]{1,0:T(8,128)(2,1)S(1)}, u32[]{:S(2)}, u32[]{:S(2)}) collective-permute-start(bf16[16,640]{1,0:T(8,128)(2,1)S(1)} %get-tuple-element.35.data_ref.own_ref), channel_id=1, source_target_pairs={{0,9},{1,8},{2,11},{3,10},{4,13},{5,12},{6,15},{7,14},{8,1},{9,0},... | collective-permute-start | bytes 61448 | tf_op jit(solution)/shard_map/ppermute | solution.py:505
  6.3 3.5 %collective-permute-start.1 = (bf16[32,640]{1,0:T(8,128)(2,1)S(1)}, bf16[32,640]{1,0:T(8,128)(2,1)S(1)}, u32[]{:S(2)}, u32[]{:S(2)}) collective-permute-start(bf16[32,640]{1,0:T(8,128)(2,1)S(1)} %constant_dynamic-update-slice_fusion.own_ref), channel_id=1, source_target_pairs={{0,5},{1,2},{2,1},{3,6},{4,7},{5,0},{6,3},{7,4},{8,11},{9,12},{10,... | collective-permute-start | bytes 122888 | tf_op jit(solution)/shard_map/ppermute | solution.py:505
  8.1 1.7 %collective-permute-start.2 = (bf16[32,640]{1,0:T(8,128)(2,1)S(1)}, bf16[32,640]{1,0:T(8,128)(2,1)S(1)}, u32[]{:S(2)}, u32[]{:S(2)}) collective-permute-start(bf16[32,640]{1,0:T(8,128)(2,1)S(1)} %constant_dynamic-update-slice_fusion.own_ref), channel_id=1, source_target_pairs={{0,1},{1,0},{2,3},{3,2},{4,5},{5,4},{6,7},{7,6},{8,9},{9,8},{10,11... | collective-permute-start | bytes 122888 | tf_op jit(solution)/shard_map/ppermute | solution.py:505
  9.8 3.9 %collective-permute-start.3 = (bf16[64,640]{1,0:T(8,128)(2,1)S(1)}, bf16[64,640]{1,0:T(8,128)(2,1)S(1)}, u32[]{:S(2)}, u32[]{:S(2)}) collective-permute-start(bf16[64,640]{1,0:T(8,128)(2,1)S(1)} %pad_maximum_fusion.own_ref.own_early), channel_id=1, source_target_pairs={{0,3},{1,4},{2,7},{3,0},{4,1},{5,6},{6,5},{7,2},{8,13},{9,10},{10,... | collective-permute-start | bytes 245768 | tf_op jit(solution)/shard_map/ppermute | solution.py:505
  11.6 1.3 %collective-permute-start.4 = (bf16[32,640]{1,0:T(8,128)(2,1)S(1)}, bf16[32,640]{1,0:T(8,128)(2,1)S(1)}, u32[]{:S(2)}, u32[]{:S(2)}) collective-permute-start(bf16[32,640]{1,0:T(8,128)(2,1)S(1)} %slice.3), channel_id=1, source_target_pairs={{0,1},{1,0},{2,3},{3,2},{4,5},{5,4},{6,7},{7,6},{8,9},{9,8},{10,11... | collective-permute-start | bytes 122888 | tf_op jit(solution)/shard_map/ppermute | solution.py:505
  13.8 1.5 %collective-permute-start.5 = (bf16[64,640]{1,0:T(8,128)(2,1)S(1)}, bf16[64,640]{1,0:T(8,128)(2,1)S(1)}, u32[]{:S(2)}, u32[]{:S(2)}) collective-permute-start(bf16[64,640]{1,0:T(8,128)(2,1)S(1)} %collective-permute-done.3.own_ref.data_ref.own_late), channel_id=1, source_target_pairs={{0,1},{1,0},{2,3},{3,2},{4,5},{5,4},{6,7},{7,6},{8,9},{9,8},{10,11... | collective-permute-start | bytes 245768 | tf_op jit(solution)/shard_map/ppermute | solution.py:505

commit v5 on v4

--- a/solution.py
+++ b/solution.py
@@ -110,12 +110,12 @@
     rows = tests_ref.shape[2]
     at = pl.ds(pl.multiple_of(col * rows, LANES), rows)
     moves = [
-        (weights_hbm, weights_ref),
+        (order_hbm, order_ref),
         (nodes_hbm, nodes_ref),
         (geom_hbm, geom_ref),
+        (tnodes_hbm, tnodes_ref),
         (excite_hbm, excite_ref),
-        (tnodes_hbm, tnodes_ref),
-        (order_hbm, order_ref),
+        (weights_hbm, weights_ref),
         (tweights_hbm.at[:, :, at], tests_ref),
     ]
     copies = [pltpu.make_async_copy(*move, arrived.at[i]) for i, move in enumerate(moves)]

time: 16.6 us -> 16.6 us (level)
  Pallas kernels: 5.53 us -> 4.96 us
  waiting for transfers between devices: 1.71 us -> 2.24 us
    ppermute x6, waiting for transfers between devices: 1.71 us -> 2.24 us  [moved(): return lax.ppermute(value, ('row', 'col'), pairs)]
    pallas_call x5, Pallas kernels: 2.76 us -> 2.24 us  [near_blocks(): pl.pallas_call(functools.partial(near_kernel if first else first_near_ker...]
  transfers between devices with their start and end apart: 6 -> 6, of which waited for: 4 -> 4; matrix products, arithmetic and copies ran while one was open for 0% -> 0% of each run, Pallas kernels for 19% -> 16%
where the time goes in v5:
time: 16.6 us; the launch traced here: 16.4 us
  starting transfers between devices  8.42 us (51%)
  Pallas kernels  4.96 us (30%)
  waiting for transfers between devices  2.24 us (13%)
  between operations  0.76 us (5%)
    ppermute x6, starting transfers between devices, moved(): return lax.ppermute(value, ('row', 'col'), pairs)  8.42 us
    ppermute x6, waiting for transfers between devices, moved(): return lax.ppermute(value, ('row', 'col'), pairs)  2.24 us
    pallas_call x5, Pallas kernels, near_blocks(): pl.pallas_call(functools.partial(near_kernel if first else first_near_ker...  2.24 us
    pallas_call x1, Pallas kernels, exchanged(): pl.pallas_call(functools.partial(last_kernel, exc, partner), out_shape=ja...  1.2 us
    pallas_call x1, Pallas kernels, packed(): pl.pallas_call(functools.partial(pack_kernel, units), out_shape=[pltpu.VM...  1.14 us
    pallas_call x2, Pallas kernels, known_rows(): pl.pallas_call(known_kernel, out_shape=pltpu.VMEM((quarter, 4 * cpd, rows...  0.39 us
  transfers between devices with their start and end apart: 6, of which 4 were waited for; matrix products, arithmetic and copies ran while one was open for 0% of the time, Pallas kernels for 16%

profile of v5, /device:TPU:0, one launch (start us, length us, event | category | flops | bytes accessed | tf_op | source)
XLA Modules:
  0.0 16.4 jit_solution(512461181874529382)
XLA Ops:
  0.0 1.1 %shard_map.91 = (bf16[16,640]{1,0:T(8,128)(2,1)S(1)}, f32[3,8,128]{2,1,0:T(8,128)S(1)}, bf16[2,192,128]{2,1,0:T(8,128)(2,1)S(1)}, s32[8]{0:T(128)S(4)}) custom-call(s32[2,9]{1,0:T(2,128)} %order_hbm.1, f32[4,16]{1,0:T(4,128)} %geom_hbm.1, bf16[16,128]{1,0:T(8,128)(2,1)} %bitcast.3, f32[3,192]{1,0:T(4,128)} %nodes_hbm.1, bf16[2,16,192]{2,1,0:T(8,128)(2,1)} %bitcast.2, ...), custom_call_target="tpu_custom_call" | custom-call | tf_op jit(solution)/shard_map/pallas_call | solution.py:455
  1.1 0.0 copy-start
  1.2 3.5 %collective-permute-start = (bf16[16,640]{1,0:T(8,128)(2,1)S(1)}, bf16[16,640]{1,0:T(8,128)(2,1)S(1)}, u32[]{:S(2)}, u32[]{:S(2)}) collective-permute-start(bf16[16,640]{1,0:T(8,128)(2,1)S(1)} %get-tuple-element.35.data_ref.own_ref), channel_id=1, source_target_pairs={{0,9},{1,8},{2,11},{3,10},{4,13},{5,12},{6,15},{7,14},{8,1},{9,0},... | collective-permute-start | bytes 61448 | tf_op jit(solution)/shard_map/ppermute | solution.py:505
  5.3 0.0 copy-done
  5.4 0.5 %shard_map.92 = (bf16[1,384,256]{2,1,0:T(8,128)(2,1)S(1)}, bf16[16,128]{1,0:T(8,128)(2,1)S(1)}, bf16[16,128]{1,0:T(8,128)(2,1)S(1)}, bf16[16,640]{1,0:T(8,128)(2,1)S(1)}, bf16[384,256]{1,0:T(8,128)(2,1)S(1)}) custom-call(f32[1]{0:T(128)S(6)} %copy.11.wave_ref, s32[8]{0:T(128)S(4)} %get-tuple-element.34.found_ref, ...), custom_call_target="tpu_custom_call" | custom-call | flops 1 | bytes 1 | tf_op jit(solution)/shard_map/pallas_call | solution.py:479
  5.9 0.3 %collective-permute-done.data_ref = bf16[16,640]{1,0:T(8,128)(2,1)S(1)} collective-permute-done((bf16[16,640]{1,0:T(8,128)(2,1)S(1)}, bf16[16,640]{1,0:T(8,128)(2,1)S(1)}, u32[]{:S(2)}, u32[]{:S(2)}) %collective-permute-start) | collective-permute-done | bytes 20512 | tf_op jit(solution)/shard_map/ppermute | solution.py:505
  6.2 1.9 %collective-permute-start.1 = (bf16[32,640]{1,0:T(8,128)(2,1)S(1)}, bf16[32,640]{1,0:T(8,128)(2,1)S(1)}, u32[]{:S(2)}, u32[]{:S(2)}) collective-permute-start(bf16[32,640]{1,0:T(8,128)(2,1)S(1)} %constant_dynamic-update-slice_fusion.own_ref), channel_id=1, source_target_pairs={{0,5},{1,2},{2,1},{3,6},{4,7},{5,0},{6,3},{7,4},{8,11},{9,12},{10,... | collective-permute-start | bytes 122888 | tf_op jit(solution)/shard_map/ppermute | solution.py:505
  8.1 0.3 %collective-permute-start.2 = (bf16[32,640]{1,0:T(8,128)(2,1)S(1)}, bf16[32,640]{1,0:T(8,128)(2,1)S(1)}, u32[]{:S(2)}, u32[]{:S(2)}) collective-permute-start(bf16[32,640]{1,0:T(8,128)(2,1)S(1)} %constant_dynamic-update-slice_fusion.own_ref), channel_id=1, source_target_pairs={{0,1},{1,0},{2,3},{3,2},{4,5},{5,4},{6,7},{7,6},{8,9},{9,8},{10,11... | collective-permute-start | bytes 122888 | tf_op jit(solution)/shard_map/ppermute | solution.py:505
  8.4 0.2 %shard_map.93 = (bf16[1,384,256]{2,1,0:T(8,128)(2,1)S(1)}, bf16[16,128]{1,0:T(8,128)(2,1)S(1)}, bf16[16,128]{1,0:T(8,128)(2,1)S(1)}, bf16[32,640]{1,0:T(8,128)(2,1)S(1)}) custom-call(f32[1]{0:T(128)S(6)} %copy.11.wave_ref, s32[8]{0:T(128)S(4)} %get-tuple-element.34.found_ref, bf16[16,640]{1,0:T(8,128)(2,1)S(1)} %collective-permute-done.data_ref, ...), custom_call_target="tpu_custom_call" | custom-call | flops 1 | bytes 1 | tf_op jit(solution)/shard_map/pallas_call | solution.py:479
  8.6 1.2 %collective-permute-done.1.data_ref = bf16[32,640]{1,0:T(8,128)(2,1)S(1)} collective-permute-done((bf16[32,640]{1,0:T(8,128)(2,1)S(1)}, bf16[32,640]{1,0:T(8,128)(2,1)S(1)}, u32[]{:S(2)}, u32[]{:S(2)}) %collective-permute-start.1) | collective-permute-done | bytes 40992 | tf_op jit(solution)/shard_map/ppermute | solution.py:505
  9.8 0.0 collective-permute-done.2.own_ref.other_ref.other_first
  9.8 1.7 %collective-permute-start.3 = (bf16[64,640]{1,0:T(8,128)(2,1)S(1)}, bf16[64,640]{1,0:T(8,128)(2,1)S(1)}, u32[]{:S(2)}, u32[]{:S(2)}) collective-permute-start(bf16[64,640]{1,0:T(8,128)(2,1)S(1)} %pad_maximum_fusion.own_ref.own_early), channel_id=1, source_target_pairs={{0,3},{1,4},{2,7},{3,0},{4,1},{5,6},{6,5},{7,2},{8,13},{9,10},{10,... | collective-permute-start | bytes 245768 | tf_op jit(solution)/shard_map/ppermute | solution.py:505
  11.5 0.5 %collective-permute-start.4 = (bf16[32,640]{1,0:T(8,128)(2,1)S(1)}, bf16[32,640]{1,0:T(8,128)(2,1)S(1)}, u32[]{:S(2)}, u32[]{:S(2)}) collective-permute-start(bf16[32,640]{1,0:T(8,128)(2,1)S(1)} %slice.3), channel_id=1, source_target_pairs={{0,1},{1,0},{2,3},{3,2},{4,5},{5,4},{6,7},{7,6},{8,9},{9,8},{10,11... | collective-permute-start | bytes 122888 | tf_op jit(solution)/shard_map/ppermute | solution.py:505
  12.0 0.2 %shard_map.96.known_early = f32[2,64,128]{2,1,0:T(8,128)S(1)} custom-call(bf16[64,640]{1,0:T(8,128)(2,1)S(1)} %pad_maximum_fusion.own_ref.own_early, bf16[32,640]{1,0:T(8,128)(2,1)S(1)} %collective-permute-done.2.own_ref.other_ref.other_first, bf16[1,384,256]{2,1,0:T(8,128)(2,1)S(1)} %get-tuple-element.49.refs_0_, ...), custom_call_target="tpu_custom_call" | custom-call | flops 1 | bytes 1 | tf_op jit(solution)/shard_map/pallas_call | solution.py:538
  12.2 0.5 %shard_map.95 = (bf16[2,384,256]{2,1,0:T(8,128)(2,1)S(1)}, bf16[64,128]{1,0:T(8,128)(2,1)S(1)}, bf16[64,128]{1,0:T(8,128)(2,1)S(1)}) custom-call(f32[1]{0:T(128)S(6)} %copy.11.wave_ref, s32[8]{0:T(128)S(4)} %get-tuple-element.34.found_ref, bf16[32,640]{1,0:T(8,128)(2,1)S(1)} %collective-permute-done.1.data_ref, ...), custom_call_target="tpu_custom_call" | custom-call | flops 1 | bytes 1 | tf_op jit(solution)/shard_map/pallas_call | solution.py:479
  12.7 0.1 collective-permute-done.4.data_ref.own_ref.other_ref.other_early
  12.9 0.2 %shard_map.94 = (bf16[2,384,256]{2,1,0:T(8,128)(2,1)S(1)}, bf16[32,128]{1,0:T(8,128)(2,1)S(1)}, bf16[32,128]{1,0:T(8,128)(2,1)S(1)}) custom-call(f32[1]{0:T(128)S(6)} %copy.11.wave_ref, s32[8]{0:T(128)S(4)} %get-tuple-element.34.found_ref, bf16[32,640]{1,0:T(8,128)(2,1)S(1)} %collective-permute-done.4.data_ref.own_ref.other_ref.other_early, ...), custom_call_target="tpu_custom_call" | custom-call | flops 1 | bytes 1 | tf_op jit(solution)/shard_map/pallas_call | solution.py:479
  13.1 0.6 %collective-permute-done.3.own_ref.data_ref.own_late = bf16[64,640]{1,0:T(8,128)(2,1)S(1)} collective-permute-done((bf16[64,640]{1,0:T(8,128)(2,1)S(1)}, bf16[64,640]{1,0:T(8,128)(2,1)S(1)}, u32[]{:S(2)}, u32[]{:S(2)}) %collective-permute-start.3) | collective-permute-done | bytes 81952 | tf_op jit(solution)/shard_map/ppermute | solution.py:505
  13.7 0.5 %collective-permute-start.5 = (bf16[64,640]{1,0:T(8,128)(2,1)S(1)}, bf16[64,640]{1,0:T(8,128)(2,1)S(1)}, u32[]{:S(2)}, u32[]{:S(2)}) collective-permute-start(bf16[64,640]{1,0:T(8,128)(2,1)S(1)} %collective-permute-done.3.own_ref.data_ref.own_late), channel_id=1, source_target_pairs={{0,1},{1,0},{2,3},{3,2},{4,5},{5,4},{6,7},{7,6},{8,9},{9,8},{10,11... | collective-permute-start | bytes 245768 | tf_op jit(solution)/shard_map/ppermute | solution.py:505
  14.2 0.8 %shard_map.98 = (bf16[2,384,256]{2,1,0:T(8,128)(2,1)S(1)}, bf16[64,128]{1,0:T(8,128)(2,1)S(1)}, bf16[64,128]{1,0:T(8,128)(2,1)S(1)}) custom-call(f32[1]{0:T(128)S(6)} %copy.11.wave_ref, s32[8]{0:T(128)S(4)} %get-tuple-element.34.found_ref, bf16[64,640]{1,0:T(8,128)(2,1)S(1)} %collective-permute-done.3.own_ref.data_ref.own_late, ...), custom_call_target="tpu_custom_call" | custom-call | flops 1 | bytes 1 | tf_op jit(solution)/shard_map/pallas_call | solution.py:479
  15.0 0.2 %shard_map.97.known_late = f32[2,64,128]{2,1,0:T(8,128)S(1)} custom-call(bf16[64,640]{1,0:T(8,128)(2,1)S(1)} %collective-permute-done.3.own_ref.data_ref.own_late, bf16[32,640]{1,0:T(8,128)(2,1)S(1)} %collective-permute-done.4.data_ref.own_ref.other_ref.other_early, bf16[2,384,256]{2,1,0:T(8,128)(2,1)S(1)} %get-tuple-element.53.refs_0_.refs_9_), custom_call_target="tpu_custom_call" | custom-call | flops 1 | bytes 1 | tf_op jit(solution)/shard_map/pallas_call | solution.py:538
  15.2 0.0 collective-permute-done.5.other_late
  15.2 1.2 %shard_map.99 = f32[128,128]{1,0:T(8,128)} custom-call(f32[1]{0:T(128)S(6)} %copy.11.wave_ref, bf16[64,640]{1,0:T(8,128)(2,1)S(1)} %pad_maximum_fusion.own_ref.own_early, bf16[64,640]{1,0:T(8,128)(2,1)S(1)} %collective-permute-done.3.own_ref.data_ref.own_late, bf16[32,640]{1,0:T(8,128)(2,1)S(1)} %collective-permute-done.2.own_ref.other_ref.other_first, ...), custom_call_target="tpu_custom_call" | custom-call | tf_op jit(solution)/shard_map/pallas_call | solution.py:557
  (4 shorter events, 0.0 us)
Async XLA Ops:
  1.1 4.2 %copy-start = (f32[6,256]{1,0:T(8,128)S(1)}, f32[6,256]{1,0:T(8,128)}, u32[]{:S(2)}) copy-start(f32[6,256]{1,0:T(8,128)} %tgeom_ref.11) | copy-start | bytes 18436
  1.2 5.1 %collective-permute-start = (bf16[16,640]{1,0:T(8,128)(2,1)S(1)}, bf16[16,640]{1,0:T(8,128)(2,1)S(1)}, u32[]{:S(2)}, u32[]{:S(2)}) collective-permute-start(bf16[16,640]{1,0:T(8,128)(2,1)S(1)} %get-tuple-element.35.data_ref.own_ref), channel_id=1, source_target_pairs={{0,9},{1,8},{2,11},{3,10},{4,13},{5,12},{6,15},{7,14},{8,1},{9,0},... | collective-permute-start | bytes 61448 | tf_op jit(solution)/shard_map/ppermute | solution.py:505
  6.2 3.5 %collective-permute-start.1 = (bf16[32,640]{1,0:T(8,128)(2,1)S(1)}, bf16[32,640]{1,0:T(8,128)(2,1)S(1)}, u32[]{:S(2)}, u32[]{:S(2)}) collective-permute-start(bf16[32,640]{1,0:T(8,128)(2,1)S(1)} %constant_dynamic-update-slice_fusion.own_ref), channel_id=1, source_target_pairs={{0,5},{1,2},{2,1},{3,6},{4,7},{5,0},{6,3},{7,4},{8,11},{9,12},{10,... | collective-permute-start | bytes 122888 | tf_op jit(solution)/shard_map/ppermute | solution.py:505
  8.1 1.7 %collective-permute-start.2 = (bf16[32,640]{1,0:T(8,128)(2,1)S(1)}, bf16[32,640]{1,0:T(8,128)(2,1)S(1)}, u32[]{:S(2)}, u32[]{:S(2)}) collective-permute-start(bf16[32,640]{1,0:T(8,128)(2,1)S(1)} %constant_dynamic-update-slice_fusion.own_ref), channel_id=1, source_target_pairs={{0,1},{1,0},{2,3},{3,2},{4,5},{5,4},{6,7},{7,6},{8,9},{9,8},{10,11... | collective-permute-start | bytes 122888 | tf_op jit(solution)/shard_map/ppermute | solution.py:505
  9.8 3.9 %collective-permute-start.3 = (bf16[64,640]{1,0:T(8,128)(2,1)S(1)}, bf16[64,640]{1,0:T(8,128)(2,1)S(1)}, u32[]{:S(2)}, u32[]{:S(2)}) collective-permute-start(bf16[64,640]{1,0:T(8,128)(2,1)S(1)} %pad_maximum_fusion.own_ref.own_early), channel_id=1, source_target_pairs={{0,3},{1,4},{2,7},{3,0},{4,1},{5,6},{6,5},{7,2},{8,13},{9,10},{10,... | collective-permute-start | bytes 245768 | tf_op jit(solution)/shard_map/ppermute | solution.py:505
  11.5 1.4 %collective-permute-start.4 = (bf16[32,640]{1,0:T(8,128)(2,1)S(1)}, bf16[32,640]{1,0:T(8,128)(2,1)S(1)}, u32[]{:S(2)}, u32[]{:S(2)}) collective-permute-start(bf16[32,640]{1,0:T(8,128)(2,1)S(1)} %slice.3), channel_id=1, source_target_pairs={{0,1},{1,0},{2,3},{3,2},{4,5},{5,4},{6,7},{7,6},{8,9},{9,8},{10,11... | collective-permute-start | bytes 122888 | tf_op jit(solution)/shard_map/ppermute | solution.py:505
  13.7 1.5 %collective-permute-start.5 = (bf16[64,640]{1,0:T(8,128)(2,1)S(1)}, bf16[64,640]{1,0:T(8,128)(2,1)S(1)}, u32[]{:S(2)}, u32[]{:S(2)}) collective-permute-start(bf16[64,640]{1,0:T(8,128)(2,1)S(1)} %collective-permute-done.3.own_ref.data_ref.own_late), channel_id=1, source_target_pairs={{0,1},{1,0},{2,3},{3,2},{4,5},{5,4},{6,7},{7,6},{8,9},{9,8},{10,11... | collective-permute-start | bytes 245768 | tf_op jit(solution)/shard_map/ppermute | solution.py:505

commit v6 on v5

--- a/solution.py
+++ b/solution.py
@@ -390,6 +390,7 @@
     main = LANES
     slots = len(partner)
     quarter = slots // 4
+    late_kern = far_rows(other_late, exc, wave_ref[0], own_targets(tgeom_ref, rows))
     own_re, own_im = weight_rows(own)
     other_re, other_im = weight_rows(other)
     slot = 0
@@ -409,7 +410,6 @@
             zim[there] = a[3 * cpd :]
             slot += 1
 
-    late_kern = far_rows(other_late, exc, wave_ref[0], own_targets(tgeom_ref, rows))
     first = other_first.shape[0]
     kern_re, kern_im = [
         jnp.concatenate(

time: 16.6 us -> 16.5 us (level)
  waiting for transfers between devices: 2.24 us -> 1.99 us
  Pallas kernels: 4.96 us -> 5.14 us
    ppermute x6, waiting for transfers between devices: 2.24 us -> 1.99 us  [moved(): return lax.ppermute(value, ('row', 'col'), pairs)]
    pallas_call x5, Pallas kernels: 2.24 us -> 2.43 us  [near_blocks(): pl.pallas_call(functools.partial(near_kernel if first else first_near_ker...]
  transfers between devices with their start and end apart: 6 -> 6, of which waited for: 4 -> 5; matrix products, arithmetic and copies ran while one was open for 0% -> 0% of each run, Pallas kernels for 16% -> 17%
where the time goes in v6:
time: 16.5 us; the launch traced here: 16.3 us
  starting transfers between devices  8.42 us (51%)
  Pallas kernels  5.14 us (31%)
  waiting for transfers between devices  1.99 us (12%)
  between operations  0.76 us (5%)
    ppermute x6, starting transfers between devices, moved(): return lax.ppermute(value, ('row', 'col'), pairs)  8.42 us
    pallas_call x5, Pallas kernels, near_blocks(): pl.pallas_call(functools.partial(near_kernel if first else first_near_ker...  2.43 us
    ppermute x6, waiting for transfers between devices, moved(): return lax.ppermute(value, ('row', 'col'), pairs)  1.99 us
    pallas_call x1, Pallas kernels, exchanged(): pl.pallas_call(functools.partial(last_kernel, exc, partner), out_shape=ja...  1.19 us
    pallas_call x1, Pallas kernels, packed(): pl.pallas_call(functools.partial(pack_kernel, units), out_shape=[pltpu.VM...  1.14 us
    pallas_call x2, Pallas kernels, known_rows(): pl.pallas_call(known_kernel, out_shape=pltpu.VMEM((quarter, 4 * cpd, rows...  0.39 us
  transfers between devices with their start and end apart: 6, of which 5 were waited for; matrix products, arithmetic and copies ran while one was open for 0% of the time, Pallas kernels for 17%

profile of v6, /device:TPU:0, one launch (start us, length us, event | category | flops | bytes accessed | tf_op | source)
XLA Modules:
  0.0 16.3 jit_solution(6729153897546226356)
XLA Ops:
  0.0 1.1 %shard_map.91 = (bf16[16,640]{1,0:T(8,128)(2,1)S(1)}, f32[3,8,128]{2,1,0:T(8,128)S(1)}, bf16[2,192,128]{2,1,0:T(8,128)(2,1)S(1)}, s32[8]{0:T(128)S(4)}) custom-call(s32[2,9]{1,0:T(2,128)} %order_hbm.1, f32[4,16]{1,0:T(4,128)} %geom_hbm.1, bf16[16,128]{1,0:T(8,128)(2,1)} %bitcast.3, f32[3,192]{1,0:T(4,128)} %nodes_hbm.1, bf16[2,16,192]{2,1,0:T(8,128)(2,1)} %bitcast.2, ...), custom_call_target="tpu_custom_call" | custom-call | tf_op jit(solution)/shard_map/pallas_call | solution.py:455
  1.1 0.0 copy-start
  1.2 3.5 %collective-permute-start = (bf16[16,640]{1,0:T(8,128)(2,1)S(1)}, bf16[16,640]{1,0:T(8,128)(2,1)S(1)}, u32[]{:S(2)}, u32[]{:S(2)}) collective-permute-start(bf16[16,640]{1,0:T(8,128)(2,1)S(1)} %get-tuple-element.35.data_ref.own_ref), channel_id=1, source_target_pairs={{0,9},{1,8},{2,11},{3,10},{4,13},{5,12},{6,15},{7,14},{8,1},{9,0},... | collective-permute-start | bytes 61448 | tf_op jit(solution)/shard_map/ppermute | solution.py:505
  5.3 0.0 copy-done
  5.4 0.7 %shard_map.92 = (bf16[1,384,256]{2,1,0:T(8,128)(2,1)S(1)}, bf16[16,128]{1,0:T(8,128)(2,1)S(1)}, bf16[16,128]{1,0:T(8,128)(2,1)S(1)}, bf16[16,640]{1,0:T(8,128)(2,1)S(1)}, bf16[384,256]{1,0:T(8,128)(2,1)S(1)}) custom-call(f32[1]{0:T(128)S(6)} %copy.11.wave_ref, s32[8]{0:T(128)S(4)} %get-tuple-element.34.found_ref, ...), custom_call_target="tpu_custom_call" | custom-call | flops 1 | bytes 1 | tf_op jit(solution)/shard_map/pallas_call | solution.py:479
  6.1 0.2 collective-permute-done.data_ref
  6.2 1.9 %collective-permute-start.1 = (bf16[32,640]{1,0:T(8,128)(2,1)S(1)}, bf16[32,640]{1,0:T(8,128)(2,1)S(1)}, u32[]{:S(2)}, u32[]{:S(2)}) collective-permute-start(bf16[32,640]{1,0:T(8,128)(2,1)S(1)} %constant_dynamic-update-slice_fusion.own_ref), channel_id=1, source_target_pairs={{0,5},{1,2},{2,1},{3,6},{4,7},{5,0},{6,3},{7,4},{8,11},{9,12},{10,... | collective-permute-start | bytes 122888 | tf_op jit(solution)/shard_map/ppermute | solution.py:505
  8.1 0.3 %collective-permute-start.2 = (bf16[32,640]{1,0:T(8,128)(2,1)S(1)}, bf16[32,640]{1,0:T(8,128)(2,1)S(1)}, u32[]{:S(2)}, u32[]{:S(2)}) collective-permute-start(bf16[32,640]{1,0:T(8,128)(2,1)S(1)} %constant_dynamic-update-slice_fusion.own_ref), channel_id=1, source_target_pairs={{0,1},{1,0},{2,3},{3,2},{4,5},{5,4},{6,7},{7,6},{8,9},{9,8},{10,11... | collective-permute-start | bytes 122888 | tf_op jit(solution)/shard_map/ppermute | solution.py:505
  8.4 0.4 %shard_map.93 = (bf16[1,384,256]{2,1,0:T(8,128)(2,1)S(1)}, bf16[16,128]{1,0:T(8,128)(2,1)S(1)}, bf16[16,128]{1,0:T(8,128)(2,1)S(1)}, bf16[32,640]{1,0:T(8,128)(2,1)S(1)}) custom-call(f32[1]{0:T(128)S(6)} %copy.11.wave_ref, s32[8]{0:T(128)S(4)} %get-tuple-element.34.found_ref, bf16[16,640]{1,0:T(8,128)(2,1)S(1)} %collective-permute-done.data_ref, ...), custom_call_target="tpu_custom_call" | custom-call | flops 1 | bytes 1 | tf_op jit(solution)/shard_map/pallas_call | solution.py:479
  8.8 0.9 %collective-permute-done.1.data_ref = bf16[32,640]{1,0:T(8,128)(2,1)S(1)} collective-permute-done((bf16[32,640]{1,0:T(8,128)(2,1)S(1)}, bf16[32,640]{1,0:T(8,128)(2,1)S(1)}, u32[]{:S(2)}, u32[]{:S(2)}) %collective-permute-start.1) | collective-permute-done | bytes 40992 | tf_op jit(solution)/shard_map/ppermute | solution.py:505
  9.8 0.0 collective-permute-done.2.own_ref.other_ref.other_first
  9.8 1.7 %collective-permute-start.3 = (bf16[64,640]{1,0:T(8,128)(2,1)S(1)}, bf16[64,640]{1,0:T(8,128)(2,1)S(1)}, u32[]{:S(2)}, u32[]{:S(2)}) collective-permute-start(bf16[64,640]{1,0:T(8,128)(2,1)S(1)} %pad_maximum_fusion.own_ref.own_early), channel_id=1, source_target_pairs={{0,3},{1,4},{2,7},{3,0},{4,1},{5,6},{6,5},{7,2},{8,13},{9,10},{10,... | collective-permute-start | bytes 245768 | tf_op jit(solution)/shard_map/ppermute | solution.py:505
  11.5 0.5 %collective-permute-start.4 = (bf16[32,640]{1,0:T(8,128)(2,1)S(1)}, bf16[32,640]{1,0:T(8,128)(2,1)S(1)}, u32[]{:S(2)}, u32[]{:S(2)}) collective-permute-start(bf16[32,640]{1,0:T(8,128)(2,1)S(1)} %slice.3), channel_id=1, source_target_pairs={{0,1},{1,0},{2,3},{3,2},{4,5},{5,4},{6,7},{7,6},{8,9},{9,8},{10,11... | collective-permute-start | bytes 122888 | tf_op jit(solution)/shard_map/ppermute | solution.py:505
  12.0 0.2 %shard_map.96.known_early = f32[2,64,128]{2,1,0:T(8,128)S(1)} custom-call(bf16[64,640]{1,0:T(8,128)(2,1)S(1)} %pad_maximum_fusion.own_ref.own_early, bf16[32,640]{1,0:T(8,128)(2,1)S(1)} %collective-permute-done.2.own_ref.other_ref.other_first, bf16[1,384,256]{2,1,0:T(8,128)(2,1)S(1)} %get-tuple-element.49.refs_0_, ...), custom_call_target="tpu_custom_call" | custom-call | flops 1 | bytes 1 | tf_op jit(solution)/shard_map/pallas_call | solution.py:538
  12.2 0.5 %shard_map.95 = (bf16[2,384,256]{2,1,0:T(8,128)(2,1)S(1)}, bf16[64,128]{1,0:T(8,128)(2,1)S(1)}, bf16[64,128]{1,0:T(8,128)(2,1)S(1)}) custom-call(f32[1]{0:T(128)S(6)} %copy.11.wave_ref, s32[8]{0:T(128)S(4)} %get-tuple-element.34.found_ref, bf16[32,640]{1,0:T(8,128)(2,1)S(1)} %collective-permute-done.1.data_ref, ...), custom_call_target="tpu_custom_call" | custom-call | flops 1 | bytes 1 | tf_op jit(solution)/shard_map/pallas_call | solution.py:479
  12.7 0.1 collective-permute-done.4.data_ref.own_ref.other_ref.other_early
  12.9 0.5 %shard_map.94 = (bf16[2,384,256]{2,1,0:T(8,128)(2,1)S(1)}, bf16[32,128]{1,0:T(8,128)(2,1)S(1)}, bf16[32,128]{1,0:T(8,128)(2,1)S(1)}) custom-call(f32[1]{0:T(128)S(6)} %copy.11.wave_ref, s32[8]{0:T(128)S(4)} %get-tuple-element.34.found_ref, bf16[32,640]{1,0:T(8,128)(2,1)S(1)} %collective-permute-done.4.data_ref.own_ref.other_ref.other_early, ...), custom_call_target="tpu_custom_call" | custom-call | flops 1 | bytes 1 | tf_op jit(solution)/shard_map/pallas_call | solution.py:479
  13.4 0.4 %collective-permute-done.3.own_ref.data_ref.own_late = bf16[64,640]{1,0:T(8,128)(2,1)S(1)} collective-permute-done((bf16[64,640]{1,0:T(8,128)(2,1)S(1)}, bf16[64,640]{1,0:T(8,128)(2,1)S(1)}, u32[]{:S(2)}, u32[]{:S(2)}) %collective-permute-start.3) | collective-permute-done | bytes 81952 | tf_op jit(solution)/shard_map/ppermute | solution.py:505
  13.7 0.5 %collective-permute-start.5 = (bf16[64,640]{1,0:T(8,128)(2,1)S(1)}, bf16[64,640]{1,0:T(8,128)(2,1)S(1)}, u32[]{:S(2)}, u32[]{:S(2)}) collective-permute-start(bf16[64,640]{1,0:T(8,128)(2,1)S(1)} %collective-permute-done.3.own_ref.data_ref.own_late), channel_id=1, source_target_pairs={{0,1},{1,0},{2,3},{3,2},{4,5},{5,4},{6,7},{7,6},{8,9},{9,8},{10,11... | collective-permute-start | bytes 245768 | tf_op jit(solution)/shard_map/ppermute | solution.py:505
  14.2 0.3 %shard_map.98 = (bf16[2,384,256]{2,1,0:T(8,128)(2,1)S(1)}, bf16[64,128]{1,0:T(8,128)(2,1)S(1)}, bf16[64,128]{1,0:T(8,128)(2,1)S(1)}) custom-call(f32[1]{0:T(128)S(6)} %copy.11.wave_ref, s32[8]{0:T(128)S(4)} %get-tuple-element.34.found_ref, bf16[64,640]{1,0:T(8,128)(2,1)S(1)} %collective-permute-done.3.own_ref.data_ref.own_late, ...), custom_call_target="tpu_custom_call" | custom-call | flops 1 | bytes 1 | tf_op jit(solution)/shard_map/pallas_call | solution.py:479
  14.5 0.2 %shard_map.97.known_late = f32[2,64,128]{2,1,0:T(8,128)S(1)} custom-call(bf16[64,640]{1,0:T(8,128)(2,1)S(1)} %collective-permute-done.3.own_ref.data_ref.own_late, bf16[32,640]{1,0:T(8,128)(2,1)S(1)} %collective-permute-done.4.data_ref.own_ref.other_ref.other_early, bf16[2,384,256]{2,1,0:T(8,128)(2,1)S(1)} %get-tuple-element.53.refs_0_.refs_9_), custom_call_target="tpu_custom_call" | custom-call | flops 1 | bytes 1 | tf_op jit(solution)/shard_map/pallas_call | solution.py:538
  14.7 0.4 %collective-permute-done.5.other_late = bf16[64,640]{1,0:T(8,128)(2,1)S(1)} collective-permute-done((bf16[64,640]{1,0:T(8,128)(2,1)S(1)}, bf16[64,640]{1,0:T(8,128)(2,1)S(1)}, u32[]{:S(2)}, u32[]{:S(2)}) %collective-permute-start.5) | collective-permute-done | bytes 81952 | tf_op jit(solution)/shard_map/ppermute | solution.py:505
  15.2 1.2 %shard_map.99 = f32[128,128]{1,0:T(8,128)} custom-call(f32[1]{0:T(128)S(6)} %copy.11.wave_ref, bf16[64,640]{1,0:T(8,128)(2,1)S(1)} %pad_maximum_fusion.own_ref.own_early, bf16[64,640]{1,0:T(8,128)(2,1)S(1)} %collective-permute-done.3.own_ref.data_ref.own_late, bf16[32,640]{1,0:T(8,128)(2,1)S(1)} %collective-permute-done.2.own_ref.other_ref.other_first, ...), custom_call_target="tpu_custom_call" | custom-call | tf_op jit(solution)/shard_map/pallas_call | solution.py:557
  (4 shorter events, 0.0 us)
Async XLA Ops:
  1.1 4.2 %copy-start = (f32[6,256]{1,0:T(8,128)S(1)}, f32[6,256]{1,0:T(8,128)}, u32[]{:S(2)}) copy-start(f32[6,256]{1,0:T(8,128)} %tgeom_ref.11) | copy-start | bytes 18436
  1.2 5.1 %collective-permute-start = (bf16[16,640]{1,0:T(8,128)(2,1)S(1)}, bf16[16,640]{1,0:T(8,128)(2,1)S(1)}, u32[]{:S(2)}, u32[]{:S(2)}) collective-permute-start(bf16[16,640]{1,0:T(8,128)(2,1)S(1)} %get-tuple-element.35.data_ref.own_ref), channel_id=1, source_target_pairs={{0,9},{1,8},{2,11},{3,10},{4,13},{5,12},{6,15},{7,14},{8,1},{9,0},... | collective-permute-start | bytes 61448 | tf_op jit(solution)/shard_map/ppermute | solution.py:505
  6.2 3.5 %collective-permute-start.1 = (bf16[32,640]{1,0:T(8,128)(2,1)S(1)}, bf16[32,640]{1,0:T(8,128)(2,1)S(1)}, u32[]{:S(2)}, u32[]{:S(2)}) collective-permute-start(bf16[32,640]{1,0:T(8,128)(2,1)S(1)} %constant_dynamic-update-slice_fusion.own_ref), channel_id=1, source_target_pairs={{0,5},{1,2},{2,1},{3,6},{4,7},{5,0},{6,3},{7,4},{8,11},{9,12},{10,... | collective-permute-start | bytes 122888 | tf_op jit(solution)/shard_map/ppermute | solution.py:505
  8.1 1.7 %collective-permute-start.2 = (bf16[32,640]{1,0:T(8,128)(2,1)S(1)}, bf16[32,640]{1,0:T(8,128)(2,1)S(1)}, u32[]{:S(2)}, u32[]{:S(2)}) collective-permute-start(bf16[32,640]{1,0:T(8,128)(2,1)S(1)} %constant_dynamic-update-slice_fusion.own_ref), channel_id=1, source_target_pairs={{0,1},{1,0},{2,3},{3,2},{4,5},{5,4},{6,7},{7,6},{8,9},{9,8},{10,11... | collective-permute-start | bytes 122888 | tf_op jit(solution)/shard_map/ppermute | solution.py:505
  9.8 3.9 %collective-permute-start.3 = (bf16[64,640]{1,0:T(8,128)(2,1)S(1)}, bf16[64,640]{1,0:T(8,128)(2,1)S(1)}, u32[]{:S(2)}, u32[]{:S(2)}) collective-permute-start(bf16[64,640]{1,0:T(8,128)(2,1)S(1)} %pad_maximum_fusion.own_ref.own_early), channel_id=1, source_target_pairs={{0,3},{1,4},{2,7},{3,0},{4,1},{5,6},{6,5},{7,2},{8,13},{9,10},{10,... | collective-permute-start | bytes 245768 | tf_op jit(solution)/shard_map/ppermute | solution.py:505
  11.5 1.4 %collective-permute-start.4 = (bf16[32,640]{1,0:T(8,128)(2,1)S(1)}, bf16[32,640]{1,0:T(8,128)(2,1)S(1)}, u32[]{:S(2)}, u32[]{:S(2)}) collective-permute-start(bf16[32,640]{1,0:T(8,128)(2,1)S(1)} %slice.3), channel_id=1, source_target_pairs={{0,1},{1,0},{2,3},{3,2},{4,5},{5,4},{6,7},{7,6},{8,9},{9,8},{10,11... | collective-permute-start | bytes 122888 | tf_op jit(solution)/shard_map/ppermute | solution.py:505
  13.7 1.4 %collective-permute-start.5 = (bf16[64,640]{1,0:T(8,128)(2,1)S(1)}, bf16[64,640]{1,0:T(8,128)(2,1)S(1)}, u32[]{:S(2)}, u32[]{:S(2)}) collective-permute-start(bf16[64,640]{1,0:T(8,128)(2,1)S(1)} %collective-permute-done.3.own_ref.data_ref.own_late), channel_id=1, source_target_pairs={{0,1},{1,0},{2,3},{3,2},{4,5},{5,4},{6,7},{7,6},{8,9},{9,8},{10,11... | collective-permute-start | bytes 245768 | tf_op jit(solution)/shard_map/ppermute | solution.py:505
